TPU v7x, 32 devices: a whole 2x2x4 slice. The times are simulated.
32 devices in a mesh: branch: 2 (over x), cluster: 16 (over z, y, core).
Axes of the slice: x: 2, y: 2, z: 4, core: 2. Of those that a mesh axis runs over, the one named last changes fastest.
Arguments:
- charges: float32 [512, 16, 256], P(('branch', 'cluster')), may hold values from -6 to 6
- coords: float32 [512, 3, 256], P(('branch', 'cluster')), may hold values from -4 to 4
- areas: float32 [512, 256], P(('branch', 'cluster')), may hold values from 0.1 to 1
- col_basis: float32 [512, 64, 256], P(('branch', 'cluster')), may hold values from -0.375 to 0.375
- row_basis: float32 [512, 64, 256], P(('branch', 'cluster')), may hold values from -0.75 to 0.75
- leaf_up: float32 [512, 64, 64], P(('branch', 'cluster')), may hold values from -0.1875 to 0.1875
- leaf_down: float32 [512, 64, 64], P(('branch', 'cluster')), may hold values from -0.75 to 0.75
- leaf_coupling: float32 [512, 4, 64, 64], P(('branch', 'cluster')), may hold values from -0.375 to 0.375
- up_transfer: float32 [2, 4, 2, 64, 64], P('branch'), may hold values from -0.5 to 0.5
- down_transfer: float32 [2, 4, 2, 64, 64], P('branch'), may hold values from -0.75 to 0.75
- sibling_coupling: float32 [2, 4, 2, 64, 64], P('branch'), may hold values from -0.75 to 0.75
- branch_coupling: float32 [2, 1, 64, 64], P('branch'), may hold values from -0.75 to 0.75
- near_list: int32 [512, 16], P(('branch', 'cluster')), may hold values from 0 to 511, as said below
- far_list: int32 [512, 4], P(('branch', 'cluster')), may hold values from 0 to 511, as said below
Outputs:
- potential: float32 [512, 16, 256], P(('branch', 'cluster'))
Inputs may be any that keep to these rules, and one draw needn't show every extreme that they name: `near_list`: row n names 16 distinct leaves of the same branch, each held by the device of leaf n or by one of its two neighbours along the cluster axis; the first entry is n itself. `far_list`: row n names 4 distinct leaves from the same window of three devices as near_list, none of them in row n of near_list.
All inputs are finite; a program needn't handle non-finite values.
Results may differ from a plain program's by a relative error of at most 0.00022.
Values sent between devices are 32-bit elements; how exact they have to be, the bound alone decides.
No kernel may reach another device: no remote copies, remote signals or barrier semaphores. Data moves between devices by JAX's collectives and lax.ppermute only.
A program may use at most 64 MiB of HBM per device.

v0:
```python
import math

import jax
import jax.numpy as jnp
from jax import lax
from jax.sharding import PartitionSpec as P

highest = lax.Precision.HIGHEST
reg_square = 0.01
inv_four_pi = 0.25 / math.pi


def padded(block, sides, width):
    for axis, dim in sides:
        count = lax.axis_size(axis)
        forward = [(i, i + 1) for i in range(count - 1)]
        backward = [(target, source) for source, target in forward]
        low = lax.ppermute(
            lax.slice_in_dim(block, block.shape[dim] - width, None, axis=dim), axis, forward
        )
        high = lax.ppermute(lax.slice_in_dim(block, 0, width, axis=dim), axis, backward)
        block = jnp.concatenate([low, block, high], axis=dim)
    return block


def from_partner(shard, axis, apart):
    return lax.ppermute(shard, axis, [(i, i ^ 1 << apart) for i in range(lax.axis_size(axis))])


def on_device(
    charges,
    coords,
    areas,
    col_basis,
    row_basis,
    leaf_up,
    leaf_down,
    leaf_coupling,
    up_transfer,
    down_transfer,
    sibling_coupling,
    branch_coupling,
    near_list,
    far_list,
):
    leaves, scenarios, panels = charges.shape
    clusters = lax.axis_size("cluster")
    levels = clusters.bit_length() - 1
    cluster_idx = lax.axis_index("cluster")
    branch_idx = lax.axis_index("branch")
    first_leaf = (branch_idx * clusters + cluster_idx) * leaves
    leaf_coef = jnp.einsum("lkp,lsp->lks", col_basis, charges, precision=highest)
    leaf_pack = jnp.concatenate([charges, coords, areas[:, None, :]], axis=1)
    source_pack = padded(leaf_pack, (("cluster", 0),), leaves)
    coef_extended = padded(leaf_coef, (("cluster", 0),), leaves)
    near_local = near_list - first_leaf + leaves

    def add_slot(slot_index, running):
        column_ids = lax.dynamic_slice_in_dim(near_local, slot_index, 1, 1)[:, 0]
        source = jnp.take(source_pack, column_ids, axis=0)
        src_charge = source[:, :scenarios]
        src_area = source[:, scenarios + 3]
        dist_square = jnp.zeros((leaves, panels, panels), jnp.float32)
        for axis_index in range(3):
            offset = coords[:, axis_index, :, None] - source[:, scenarios + axis_index, None, :]
            dist_square = dist_square + offset * offset
        kernel = src_area[:, None, :] * inv_four_pi / jnp.sqrt(dist_square + reg_square)
        return running + jnp.einsum("lpq,lsq->lsp", kernel, src_charge, precision=highest)

    near_part = lax.fori_loop(
        0, near_list.shape[1], add_slot, jnp.zeros((leaves, scenarios, panels), jnp.float32)
    )
    far_local = far_list - first_leaf + leaves
    far_coef = jnp.take(coef_extended, far_local, axis=0)
    leaf_local = jnp.einsum("ljac,ljcs->las", leaf_coupling, far_coef, precision=highest)
    node_coef = jnp.einsum("lac,lcs->as", leaf_up, leaf_coef, precision=highest)
    up_mats = up_transfer[0]
    siblings = []
    current = node_coef
    for level_index in range(levels):
        sibling = from_partner(current, "cluster", level_index)
        parity = cluster_idx >> level_index & 1
        left_child = jnp.where(parity == 0, current, sibling)
        right_child = jnp.where(parity == 0, sibling, current)
        current = jnp.dot(up_mats[level_index, 0], left_child, precision=highest) + jnp.dot(
            up_mats[level_index, 1], right_child, precision=highest
        )
        siblings.append(sibling)
    branch_roots = lax.all_gather(current[None], "branch", axis=0, tiled=True)
    branch_count = branch_roots.shape[0]
    partner_ids = (branch_idx + 1 + jnp.arange(branch_count - 1)) % branch_count
    partner_roots = jnp.take(branch_roots, partner_ids, axis=0)
    downward = jnp.einsum("iac,ics->as", branch_coupling[0], partner_roots, precision=highest)
    for level_index in reversed(range(levels)):
        parity = cluster_idx >> level_index & 1
        sib_mat = jnp.take(sibling_coupling[0, level_index], parity, axis=0)
        down_mat = jnp.take(down_transfer[0, level_index], parity, axis=0)
        downward = jnp.dot(sib_mat, siblings[level_index], precision=highest) + jnp.dot(
            down_mat, downward, precision=highest
        )
    leaf_total = leaf_local + jnp.einsum("lac,cs->las", leaf_down, downward, precision=highest)
    return jnp.einsum("lkp,lks->lsp", row_basis, leaf_total, precision=highest) + near_part


def solution(mesh):
    in_specs = (
        P(("branch", "cluster"), None, None),
        P(("branch", "cluster"), None, None),
        P(("branch", "cluster"), None),
        P(("branch", "cluster"), None, None),
        P(("branch", "cluster"), None, None),
        P(("branch", "cluster"), None, None),
        P(("branch", "cluster"), None, None),
        P(("branch", "cluster"), None, None, None),
        P("branch", None, None, None, None),
        P("branch", None, None, None, None),
        P("branch", None, None, None, None),
        P("branch", None, None, None),
        P(("branch", "cluster"), None),
        P(("branch", "cluster"), None),
    )
    out_specs = P(("branch", "cluster"), None, None)
    return jax.shard_map(
        on_device, mesh=mesh, in_specs=in_specs, out_specs=out_specs, check_vma=False
    )
```

profile of v0, /device:TPU:0, one launch (start us, length us, event | category | flops | bytes accessed | tf_op | source)
XLA Modules:
  0.0 185.1 jit_solution(9313026574016319406)
XLA Ops:
  0.0 2.4 %fusion.122 = f32[16,64,16]{1,2,0:T(8,128)S(1)} fusion(f32[16,64,256]{2,1,0:T(8,128)} %param.21, f32[16,16,256]{2,1,0:T(8,128)} %param.18), kind=kOutput, calls=%fused_computation.169 | convolution fusion | flops 50331648 | bytes 1376256 | tf_op jit(solution)/shard_map/lkp,lsp->lks/dot_general | solution.py:52
  2.5 3.0 %collective-permute-start = (f32[16,64,16]{1,2,0:T(8,128)S(1)}, f32[16,64,16]{1,2,0:T(8,128)}, u32[]{:S(2)}, u32[]{:S(2)}) collective-permute-start(f32[16,64,16]{1,2,0:T(8,128)S(1)} %fusion.122), channel_id=1, source_target_pairs={{0,1},{1,2},{2,3},{3,4},{4,5},{5,6},{6,7},{7,8},{8,9},{9,10},{10,1... | collective-permute-start | bytes 196616 | tf_op jit(solution)/shard_map/ppermute | solution.py:18
  10.1 5.3 %collective-permute-start.6 = (f32[16,20,256]{2,1,0:T(8,128)}, f32[16,20,256]{2,1,0:T(8,128)}, u32[]{:S(2)}, u32[]{:S(2)}) collective-permute-start(f32[16,20,256]{2,1,0:T(8,128)} %pad_maximum_fusion.2), channel_id=1, source_target_pairs={{0,1},{1,2},{2,3},{3,4},{4,5},{5,6},{6,7},{7,8},{8,9},{9,10},{10,1... | collective-permute-start | bytes 983048 | tf_op jit(solution)/shard_map/ppermute | solution.py:18
  20.0 2.5 %collective-permute-start.3 = (f32[64,16]{0,1:T(8,128)S(1)}, f32[64,16]{0,1:T(8,128)S(1)}, u32[]{:S(2)}, u32[]{:S(2)}) collective-permute-start(f32[64,16]{0,1:T(8,128)S(1)} %fusion.29), channel_id=1, source_target_pairs={{0,2},{1,3},{2,0},{3,1},{4,6},{5,7},{6,4},{7,5},{8,10},{9,11},{10,... | collective-permute-start | bytes 12296 | tf_op jit(solution)/shard_map/ppermute | solution.py:27
  22.4 3.6 %collective-permute-done.3 = f32[64,16]{0,1:T(8,128)S(1)} collective-permute-done((f32[64,16]{0,1:T(8,128)S(1)}, f32[64,16]{0,1:T(8,128)S(1)}, u32[]{:S(2)}, u32[]{:S(2)}) %collective-permute-start.3) | collective-permute-done | bytes 4128 | tf_op jit(solution)/shard_map/ppermute | solution.py:27
  26.3 3.9 %collective-permute-start.4 = (f32[64,16]{0,1:T(8,128)S(1)}, f32[64,16]{0,1:T(8,128)S(1)}, u32[]{:S(2)}, u32[]{:S(2)}) collective-permute-start(f32[64,16]{0,1:T(8,128)S(1)} %fusion.28), channel_id=1, source_target_pairs={{0,4},{1,5},{2,6},{3,7},{4,0},{5,1},{6,2},{7,3},{8,12},{9,13},{10,... | collective-permute-start | bytes 12296 | tf_op jit(solution)/shard_map/ppermute | solution.py:27
  32.2 3.0 %collective-permute-start.5 = (f32[64,16]{0,1:T(8,128)S(1)}, f32[64,16]{0,1:T(8,128)S(1)}, u32[]{:S(2)}, u32[]{:S(2)}) collective-permute-start(f32[64,16]{0,1:T(8,128)S(1)} %fusion.27), channel_id=1, source_target_pairs={{0,8},{1,9},{2,10},{3,11},{4,12},{5,13},{6,14},{7,15},{8,0},{9,1},... | collective-permute-start | bytes 12296 | tf_op jit(solution)/shard_map/ppermute | solution.py:27
  37.2 4.4 %all-gather.1 = f32[2,64,16]{1,2,0:T(8,128)S(1)} all-gather(f32[1,64,16]{1,2,0:T(8,128)S(1)} %fusion.26), channel_id=2, replica_groups=mesh['branch'=2,'cluster'=16] {'branch'}, dimensions={0}, use_global_device_ids=true | all-gather | bytes 12288 | tf_op jit(solution)/shard_map/all_gather | solution.py:89
  49.5 2.3 %pad_maximum_fusion = f32[48,20,256]{2,1,0:T(8,128)} fusion(f32[16,20,256]{2,1,0:T(8,128)} %collective-permute-done.7, f32[16,1,256]{2,1,0:T(1,128)S(1)} %broadcast_in_dim.70, f32[16,3,256]{2,1,0:T(4,128)S(1)} %copy.26, f32[16,16,256]{2,1,0:T(8,128)S(1)} %copy-done.1, f32[16,20,256]{2,1,0:T(8,128)} %collective-permute-done.6), kind=kLoop, calls=%fused_computation.37 | loop fusion | flops 983040 | bytes 1966080 | tf_op jit(solution)/shard_map/concatenate | solution.py:22
  51.8 132.6 %while.16 = (s32[]{:T(128)}, f32[16,16,256]{2,1,0:T(8,128)S(1)}, s32[16,16]{0,1:T(8,128)S(1)}, f32[48,20,256]{2,1,0:T(8,128)}, f32[16,3,256]{2,0,1:T(8,128)S(1)}, /*index=5*/s32[]{:T(128)}, s32[]{:T(128)}) while((s32[]{:T(128)}, f32[16,16,256]{2,1,0:T(8,128)S(1)}, s32[16,16]{0,1:T(8,128)S(1)}, f32[48,20,256]{2,1,0:T(8,128)}, ...), condition=%wide.region_1.3_spmd.clone, body=%wide.region_0.2_spmd.clone.sunk | while | flops 212030560 | bytes 2576763 | solution.py:70
  51.8 1.8 gather_fusion
  53.9 6.2 %fusion.146 = f32[16,16,256]{2,1,0:T(8,128)S(1)} fusion(f32[16,256]{1,0:T(8,128)S(1)} %get-tuple-element.222, f32[16,256]{1,0:T(8,128)S(1)} %get-tuple-element.223, f32[16,256]{1,0:T(8,128)S(1)} %get-tuple-element.224, f32[16,256]{1,0:T(8,128)S(1)} %get-tuple-element.225, f32[16,256]{1,0:T(8,128)S(1)} %get-tuple-element.228, ...), kind=kOutput, calls=%fused_computation.22.clone.1 | convolution fusion | flops 211943424 | bytes 901121 | tf_op jit(solution)/shard_map/while/body/eval_jaxpr/lpq,lsq->lsp/dot_general | solution.py:68
  60.1 1.8 gather_fusion
  62.1 6.2 %fusion.146 = f32[16,16,256]{2,1,0:T(8,128)S(1)} fusion(f32[16,256]{1,0:T(8,128)S(1)} %get-tuple-element.222, f32[16,256]{1,0:T(8,128)S(1)} %get-tuple-element.223, f32[16,256]{1,0:T(8,128)S(1)} %get-tuple-element.224, f32[16,256]{1,0:T(8,128)S(1)} %get-tuple-element.225, f32[16,256]{1,0:T(8,128)S(1)} %get-tuple-element.228, ...), kind=kOutput, calls=%fused_computation.22.clone.1 | convolution fusion | flops 211943424 | bytes 901121 | tf_op jit(solution)/shard_map/while/body/eval_jaxpr/lpq,lsq->lsp/dot_general | solution.py:68
  70.4 6.2 %fusion.146 = f32[16,16,256]{2,1,0:T(8,128)S(1)} fusion(f32[16,256]{1,0:T(8,128)S(1)} %get-tuple-element.222, f32[16,256]{1,0:T(8,128)S(1)} %get-tuple-element.223, f32[16,256]{1,0:T(8,128)S(1)} %get-tuple-element.224, f32[16,256]{1,0:T(8,128)S(1)} %get-tuple-element.225, f32[16,256]{1,0:T(8,128)S(1)} %get-tuple-element.228, ...), kind=kOutput, calls=%fused_computation.22.clone.1 | convolution fusion | flops 211943424 | bytes 901121 | tf_op jit(solution)/shard_map/while/body/eval_jaxpr/lpq,lsq->lsp/dot_general | solution.py:68
  76.7 1.8 gather_fusion
  78.7 6.2 %fusion.146 = f32[16,16,256]{2,1,0:T(8,128)S(1)} fusion(f32[16,256]{1,0:T(8,128)S(1)} %get-tuple-element.222, f32[16,256]{1,0:T(8,128)S(1)} %get-tuple-element.223, f32[16,256]{1,0:T(8,128)S(1)} %get-tuple-element.224, f32[16,256]{1,0:T(8,128)S(1)} %get-tuple-element.225, f32[16,256]{1,0:T(8,128)S(1)} %get-tuple-element.228, ...), kind=kOutput, calls=%fused_computation.22.clone.1 | convolution fusion | flops 211943424 | bytes 901121 | tf_op jit(solution)/shard_map/while/body/eval_jaxpr/lpq,lsq->lsp/dot_general | solution.py:68
  87.0 6.2 %fusion.146 = f32[16,16,256]{2,1,0:T(8,128)S(1)} fusion(f32[16,256]{1,0:T(8,128)S(1)} %get-tuple-element.222, f32[16,256]{1,0:T(8,128)S(1)} %get-tuple-element.223, f32[16,256]{1,0:T(8,128)S(1)} %get-tuple-element.224, f32[16,256]{1,0:T(8,128)S(1)} %get-tuple-element.225, f32[16,256]{1,0:T(8,128)S(1)} %get-tuple-element.228, ...), kind=kOutput, calls=%fused_computation.22.clone.1 | convolution fusion | flops 211943424 | bytes 901121 | tf_op jit(solution)/shard_map/while/body/eval_jaxpr/lpq,lsq->lsp/dot_general | solution.py:68
  93.2 1.8 gather_fusion
  95.3 6.2 %fusion.146 = f32[16,16,256]{2,1,0:T(8,128)S(1)} fusion(f32[16,256]{1,0:T(8,128)S(1)} %get-tuple-element.222, f32[16,256]{1,0:T(8,128)S(1)} %get-tuple-element.223, f32[16,256]{1,0:T(8,128)S(1)} %get-tuple-element.224, f32[16,256]{1,0:T(8,128)S(1)} %get-tuple-element.225, f32[16,256]{1,0:T(8,128)S(1)} %get-tuple-element.228, ...), kind=kOutput, calls=%fused_computation.22.clone.1 | convolution fusion | flops 211943424 | bytes 901121 | tf_op jit(solution)/shard_map/while/body/eval_jaxpr/lpq,lsq->lsp/dot_general | solution.py:68
  101.5 1.8 gather_fusion
  103.6 6.2 %fusion.146 = f32[16,16,256]{2,1,0:T(8,128)S(1)} fusion(f32[16,256]{1,0:T(8,128)S(1)} %get-tuple-element.222, f32[16,256]{1,0:T(8,128)S(1)} %get-tuple-element.223, f32[16,256]{1,0:T(8,128)S(1)} %get-tuple-element.224, f32[16,256]{1,0:T(8,128)S(1)} %get-tuple-element.225, f32[16,256]{1,0:T(8,128)S(1)} %get-tuple-element.228, ...), kind=kOutput, calls=%fused_computation.22.clone.1 | convolution fusion | flops 211943424 | bytes 901121 | tf_op jit(solution)/shard_map/while/body/eval_jaxpr/lpq,lsq->lsp/dot_general | solution.py:68
  111.9 6.2 %fusion.146 = f32[16,16,256]{2,1,0:T(8,128)S(1)} fusion(f32[16,256]{1,0:T(8,128)S(1)} %get-tuple-element.222, f32[16,256]{1,0:T(8,128)S(1)} %get-tuple-element.223, f32[16,256]{1,0:T(8,128)S(1)} %get-tuple-element.224, f32[16,256]{1,0:T(8,128)S(1)} %get-tuple-element.225, f32[16,256]{1,0:T(8,128)S(1)} %get-tuple-element.228, ...), kind=kOutput, calls=%fused_computation.22.clone.1 | convolution fusion | flops 211943424 | bytes 901121 | tf_op jit(solution)/shard_map/while/body/eval_jaxpr/lpq,lsq->lsp/dot_general | solution.py:68
  118.1 1.8 gather_fusion
  120.2 6.2 %fusion.146 = f32[16,16,256]{2,1,0:T(8,128)S(1)} fusion(f32[16,256]{1,0:T(8,128)S(1)} %get-tuple-element.222, f32[16,256]{1,0:T(8,128)S(1)} %get-tuple-element.223, f32[16,256]{1,0:T(8,128)S(1)} %get-tuple-element.224, f32[16,256]{1,0:T(8,128)S(1)} %get-tuple-element.225, f32[16,256]{1,0:T(8,128)S(1)} %get-tuple-element.228, ...), kind=kOutput, calls=%fused_computation.22.clone.1 | convolution fusion | flops 211943424 | bytes 901121 | tf_op jit(solution)/shard_map/while/body/eval_jaxpr/lpq,lsq->lsp/dot_general | solution.py:68
  128.5 6.2 %fusion.146 = f32[16,16,256]{2,1,0:T(8,128)S(1)} fusion(f32[16,256]{1,0:T(8,128)S(1)} %get-tuple-element.222, f32[16,256]{1,0:T(8,128)S(1)} %get-tuple-element.223, f32[16,256]{1,0:T(8,128)S(1)} %get-tuple-element.224, f32[16,256]{1,0:T(8,128)S(1)} %get-tuple-element.225, f32[16,256]{1,0:T(8,128)S(1)} %get-tuple-element.228, ...), kind=kOutput, calls=%fused_computation.22.clone.1 | convolution fusion | flops 211943424 | bytes 901121 | tf_op jit(solution)/shard_map/while/body/eval_jaxpr/lpq,lsq->lsp/dot_general | solution.py:68
  136.7 6.2 %fusion.146 = f32[16,16,256]{2,1,0:T(8,128)S(1)} fusion(f32[16,256]{1,0:T(8,128)S(1)} %get-tuple-element.222, f32[16,256]{1,0:T(8,128)S(1)} %get-tuple-element.223, f32[16,256]{1,0:T(8,128)S(1)} %get-tuple-element.224, f32[16,256]{1,0:T(8,128)S(1)} %get-tuple-element.225, f32[16,256]{1,0:T(8,128)S(1)} %get-tuple-element.228, ...), kind=kOutput, calls=%fused_computation.22.clone.1 | convolution fusion | flops 211943424 | bytes 901121 | tf_op jit(solution)/shard_map/while/body/eval_jaxpr/lpq,lsq->lsp/dot_general | solution.py:68
  145.0 6.2 %fusion.146 = f32[16,16,256]{2,1,0:T(8,128)S(1)} fusion(f32[16,256]{1,0:T(8,128)S(1)} %get-tuple-element.222, f32[16,256]{1,0:T(8,128)S(1)} %get-tuple-element.223, f32[16,256]{1,0:T(8,128)S(1)} %get-tuple-element.224, f32[16,256]{1,0:T(8,128)S(1)} %get-tuple-element.225, f32[16,256]{1,0:T(8,128)S(1)} %get-tuple-element.228, ...), kind=kOutput, calls=%fused_computation.22.clone.1 | convolution fusion | flops 211943424 | bytes 901121 | tf_op jit(solution)/shard_map/while/body/eval_jaxpr/lpq,lsq->lsp/dot_general | solution.py:68
  153.3 6.2 %fusion.146 = f32[16,16,256]{2,1,0:T(8,128)S(1)} fusion(f32[16,256]{1,0:T(8,128)S(1)} %get-tuple-element.222, f32[16,256]{1,0:T(8,128)S(1)} %get-tuple-element.223, f32[16,256]{1,0:T(8,128)S(1)} %get-tuple-element.224, f32[16,256]{1,0:T(8,128)S(1)} %get-tuple-element.225, f32[16,256]{1,0:T(8,128)S(1)} %get-tuple-element.228, ...), kind=kOutput, calls=%fused_computation.22.clone.1 | convolution fusion | flops 211943424 | bytes 901121 | tf_op jit(solution)/shard_map/while/body/eval_jaxpr/lpq,lsq->lsp/dot_general | solution.py:68
  161.6 6.2 %fusion.146 = f32[16,16,256]{2,1,0:T(8,128)S(1)} fusion(f32[16,256]{1,0:T(8,128)S(1)} %get-tuple-element.222, f32[16,256]{1,0:T(8,128)S(1)} %get-tuple-element.223, f32[16,256]{1,0:T(8,128)S(1)} %get-tuple-element.224, f32[16,256]{1,0:T(8,128)S(1)} %get-tuple-element.225, f32[16,256]{1,0:T(8,128)S(1)} %get-tuple-element.228, ...), kind=kOutput, calls=%fused_computation.22.clone.1 | convolution fusion | flops 211943424 | bytes 901121 | tf_op jit(solution)/shard_map/while/body/eval_jaxpr/lpq,lsq->lsp/dot_general | solution.py:68
  169.9 6.2 %fusion.146 = f32[16,16,256]{2,1,0:T(8,128)S(1)} fusion(f32[16,256]{1,0:T(8,128)S(1)} %get-tuple-element.222, f32[16,256]{1,0:T(8,128)S(1)} %get-tuple-element.223, f32[16,256]{1,0:T(8,128)S(1)} %get-tuple-element.224, f32[16,256]{1,0:T(8,128)S(1)} %get-tuple-element.225, f32[16,256]{1,0:T(8,128)S(1)} %get-tuple-element.228, ...), kind=kOutput, calls=%fused_computation.22.clone.1 | convolution fusion | flops 211943424 | bytes 901121 | tf_op jit(solution)/shard_map/while/body/eval_jaxpr/lpq,lsq->lsp/dot_general | solution.py:68
  178.2 6.2 %fusion.146 = f32[16,16,256]{2,1,0:T(8,128)S(1)} fusion(f32[16,256]{1,0:T(8,128)S(1)} %get-tuple-element.222, f32[16,256]{1,0:T(8,128)S(1)} %get-tuple-element.223, f32[16,256]{1,0:T(8,128)S(1)} %get-tuple-element.224, f32[16,256]{1,0:T(8,128)S(1)} %get-tuple-element.225, f32[16,256]{1,0:T(8,128)S(1)} %get-tuple-element.228, ...), kind=kOutput, calls=%fused_computation.22.clone.1 | convolution fusion | flops 211943424 | bytes 901121 | tf_op jit(solution)/shard_map/while/body/eval_jaxpr/lpq,lsq->lsp/dot_general | solution.py:68
  (191 shorter events, 43.4 us)
Async XLA Ops:
  0.0 45.6 %copy-start = (f32[16,4,64,64]{3,2,1,0:T(8,128)S(1)}, f32[16,4,64,64]{3,2,1,0:T(8,128)}, u32[]{:S(2)}) copy-start(f32[16,4,64,64]{3,2,1,0:T(8,128)} %param.25) | copy-start | bytes 3145732
  0.0 16.7 %copy-start.5 = (f32[16,64,64]{2,1,0:T(8,128)S(1)}, f32[16,64,64]{2,1,0:T(8,128)}, u32[]{:S(2)}) copy-start(f32[16,64,64]{2,1,0:T(8,128)} %param.23) | copy-start | bytes 786436
  0.0 18.8 %copy-start.7 = (f32[1,4,2,64,64]{4,3,2,1,0:T(8,128)S(1)}, f32[1,4,2,64,64]{4,3,2,1,0:T(8,128)}, u32[]{:S(2)}) copy-start(f32[1,4,2,64,64]{4,3,2,1,0:T(8,128)} %param.27) | copy-start | bytes 393220
  0.0 18.8 %copy-start.8 = (f32[1,4,2,64,64]{4,3,2,1,0:T(8,128)S(1)}, f32[1,4,2,64,64]{4,3,2,1,0:T(8,128)}, u32[]{:S(2)}) copy-start(f32[1,4,2,64,64]{4,3,2,1,0:T(8,128)} %param.28) | copy-start | bytes 393220
  0.0 18.9 %copy-start.9 = (s32[16,16]{1,0:T(8,128)S(1)}, s32[16,16]{1,0:T(8,128)}, u32[]{:S(2)}) copy-start(s32[16,16]{1,0:T(8,128)} %param.30) | copy-start | bytes 3076
  0.0 19.6 %copy-start.6 = (f32[1,4,2,64,64]{4,3,2,1,0:T(8,128)S(1)}, f32[1,4,2,64,64]{4,3,2,1,0:T(8,128)}, u32[]{:S(2)}) copy-start(f32[1,4,2,64,64]{4,3,2,1,0:T(8,128)} %param.26) | copy-start | bytes 393220
  0.0 30.2 %copy-start.10 = (s32[16,4]{0,1:T(4,128)S(1)}, s32[16,4]{0,1:T(4,128)}, u32[]{:S(2)}) copy-start(s32[16,4]{0,1:T(4,128)} %param.31) | copy-start | bytes 772
  2.5 41.5 %collective-permute-start = (f32[16,64,16]{1,2,0:T(8,128)S(1)}, f32[16,64,16]{1,2,0:T(8,128)}, u32[]{:S(2)}, u32[]{:S(2)}) collective-permute-start(f32[16,64,16]{1,2,0:T(8,128)S(1)} %fusion.122), channel_id=1, source_target_pairs={{0,1},{1,2},{2,3},{3,4},{4,5},{5,6},{6,7},{7,8},{8,9},{9,10},{10,1... | collective-permute-start | bytes 196616 | tf_op jit(solution)/shard_map/ppermute | solution.py:18
  5.5 38.5 %collective-permute-start.1 = (f32[16,64,16]{1,2,0:T(8,128)S(1)}, f32[16,64,16]{1,2,0:T(8,128)}, u32[]{:S(2)}, u32[]{:S(2)}) collective-permute-start(f32[16,64,16]{1,2,0:T(8,128)S(1)} %fusion.122), channel_id=1, source_target_pairs={{1,0},{2,1},{3,2},{4,3},{5,4},{6,5},{7,6},{8,7},{9,8},{10,9},{11,1... | collective-permute-start | bytes 196616 | tf_op jit(solution)/shard_map/ppermute | solution.py:21
  10.1 39.4 %collective-permute-start.6 = (f32[16,20,256]{2,1,0:T(8,128)}, f32[16,20,256]{2,1,0:T(8,128)}, u32[]{:S(2)}, u32[]{:S(2)}) collective-permute-start(f32[16,20,256]{2,1,0:T(8,128)} %pad_maximum_fusion.2), channel_id=1, source_target_pairs={{0,1},{1,2},{2,3},{3,4},{4,5},{5,6},{6,7},{7,8},{8,9},{9,10},{10,1... | collective-permute-start | bytes 983048 | tf_op jit(solution)/shard_map/ppermute | solution.py:18
  15.4 34.1 %collective-permute-start.7 = (f32[16,20,256]{2,1,0:T(8,128)}, f32[16,20,256]{2,1,0:T(8,128)}, u32[]{:S(2)}, u32[]{:S(2)}) collective-permute-start(f32[16,20,256]{2,1,0:T(8,128)} %pad_maximum_fusion.2), channel_id=1, source_target_pairs={{1,0},{2,1},{3,2},{4,3},{5,4},{6,5},{7,6},{8,7},{9,8},{10,9},{11,1... | collective-permute-start | bytes 983048 | tf_op jit(solution)/shard_map/ppermute | solution.py:21
  17.2 2.4 %collective-permute-start.2 = (f32[64,16]{0,1:T(8,128)S(1)}, f32[64,16]{0,1:T(8,128)S(1)}, u32[]{:S(2)}, u32[]{:S(2)}) collective-permute-start(f32[64,16]{0,1:T(8,128)S(1)} %convolution_bitcast_fusion.2), channel_id=1, source_target_pairs={{0,1},{1,0},{2,3},{3,2},{4,5},{5,4},{6,7},{7,6},{8,9},{9,8},{10,11... | collective-permute-start | bytes 12296 | tf_op jit(solution)/shard_map/ppermute | solution.py:27
  20.0 6.0 %collective-permute-start.3 = (f32[64,16]{0,1:T(8,128)S(1)}, f32[64,16]{0,1:T(8,128)S(1)}, u32[]{:S(2)}, u32[]{:S(2)}) collective-permute-start(f32[64,16]{0,1:T(8,128)S(1)} %fusion.29), channel_id=1, source_target_pairs={{0,2},{1,3},{2,0},{3,1},{4,6},{5,7},{6,4},{7,5},{8,10},{9,11},{10,... | collective-permute-start | bytes 12296 | tf_op jit(solution)/shard_map/ppermute | solution.py:27
  26.3 5.6 %collective-permute-start.4 = (f32[64,16]{0,1:T(8,128)S(1)}, f32[64,16]{0,1:T(8,128)S(1)}, u32[]{:S(2)}, u32[]{:S(2)}) collective-permute-start(f32[64,16]{0,1:T(8,128)S(1)} %fusion.28), channel_id=1, source_target_pairs={{0,4},{1,5},{2,6},{3,7},{4,0},{5,1},{6,2},{7,3},{8,12},{9,13},{10,... | collective-permute-start | bytes 12296 | tf_op jit(solution)/shard_map/ppermute | solution.py:27
  32.2 4.7 %collective-permute-start.5 = (f32[64,16]{0,1:T(8,128)S(1)}, f32[64,16]{0,1:T(8,128)S(1)}, u32[]{:S(2)}, u32[]{:S(2)}) collective-permute-start(f32[64,16]{0,1:T(8,128)S(1)} %fusion.27), channel_id=1, source_target_pairs={{0,8},{1,9},{2,10},{3,11},{4,12},{5,13},{6,14},{7,15},{8,0},{9,1},... | collective-permute-start | bytes 12296 | tf_op jit(solution)/shard_map/ppermute | solution.py:27
  45.6 1.9 %copy-start.4 = (f32[16,64,64]{2,1,0:T(8,128)S(1)}, f32[16,64,64]{2,1,0:T(8,128)}, u32[]{:S(2)}) copy-start(f32[16,64,64]{2,1,0:T(8,128)} %param.24) | copy-start | bytes 786436
  45.6 3.2 %copy-start.3 = (f32[16,64,256]{2,1,0:T(8,128)S(1)}, f32[16,64,256]{2,1,0:T(8,128)}, u32[]{:S(2)}) copy-start(f32[16,64,256]{2,1,0:T(8,128)} %param.22) | copy-start | bytes 3145732
  45.6 3.9 %copy-start.1 = (f32[16,16,256]{2,1,0:T(8,128)S(1)}, f32[16,16,256]{2,1,0:T(8,128)}, u32[]{:S(2)}) copy-start(f32[16,16,256]{2,1,0:T(8,128)} %param.18) | copy-start | bytes 786436
  47.5 4.3 %copy-start.2 = (f32[16,3,256]{2,0,1:T(8,128)S(1)}, f32[16,3,256]{2,0,1:T(8,128)}, u32[]{:S(2)}) copy-start(f32[16,3,256]{2,0,1:T(8,128)} %param.19) | copy-start | bytes 147460
where the time goes:
time: 186 us; the launch traced here: 185 us
  matrix products  109 us (59%)
  local copies, waits for them, and re-layouts  32.4 us (17%)
  starting transfers between devices  21.9 us (12%)
  other arithmetic  8.54 us (5%)
  waiting for transfers between devices  7.28 us (4%)
  blocking collectives  4.39 us (2%)
    dot_general x16, matrix products, add_slot(): jnp.einsum('lpq,lsq->lsp', kernel, src_charge, precision=highest)  99.1 us
    gather x16, local copies, waits for them, and re-layouts, add_slot(): source = jnp.take(source_pack, column_ids, axis=0)  29.5 us
    ppermute x4, starting transfers between devices, from_partner(): lax.ppermute(shard, axis, [(i, i ^ 1 << apart) for i in range(lax.axis_si...  11 us
    ppermute x2, starting transfers between devices, padded(): lax.ppermute(lax.slice_in_dim(block, block.shape[dim] - width, None, axis...  8.34 us
    ppermute x4, waiting for transfers between devices, from_partner(): lax.ppermute(shard, axis, [(i, i ^ 1 << apart) for i in range(lax.axis_si...  7.25 us
    all_gather x1, blocking collectives, on_device(): branch_roots = lax.all_gather(current[None], 'branch', axis=0, tiled=True)  4.39 us
  transfers between devices with their start and end apart: 8, of which 4 were waited for; matrix products, arithmetic and copies ran while one was open for 7% of the time, Pallas kernels for 0%

commit v1 on v0

v1 whole, which is shorter than its diff:
```python
import functools
import math

import jax
import jax.numpy as jnp
from jax import lax
from jax.experimental import pallas as pl
from jax.experimental.pallas import tpu as pltpu
from jax.sharding import PartitionSpec as P

f32, bf16 = jnp.float32, jnp.bfloat16
reg_square = 0.01
inv_four_pi = 0.25 / math.pi
dims = 3
ahead = 4
chunk = 2 * ahead
vmem = pl.BlockSpec(memory_space=pltpu.VMEM)
smem = pl.BlockSpec(memory_space=pltpu.SMEM)
params = pltpu.CompilerParams(vmem_limit_bytes=20 * 2**20)
depth = 32


def split(x):
    high = x.astype(bf16)
    return high, (x - high.astype(f32)).astype(bf16)


def split_three(x):
    high, rest = x.astype(bf16), None
    rest = x - high.astype(f32)
    middle = rest.astype(bf16)
    return high, middle, (rest - middle.astype(f32)).astype(bf16)


def dot_split(a, b, contract):
    rows = a.shape[0]
    a_high, a_low = split(a)
    b_high, b_low = split(b)
    numbers = (((1,), (contract,)), ((), ()))
    first = lax.dot_general(
        jnp.concatenate([a_high, a_low], axis=0), b_high, numbers, preferred_element_type=f32
    )
    second = lax.dot_general(a_high, b_low, numbers, preferred_element_type=f32)
    return first[:rows] + first[rows:] + second


def pieces_of(coords, source):
    norm = coords[0] * coords[0] + coords[1] * coords[1] + coords[2] * coords[2]
    if not source:
        norm = norm + reg_square
        coords = [-2.0 * c for c in coords]
    rows = []
    for c in coords:
        high, middle, low = split_three(c)
        rows += [high, middle, high, low, high, middle] if source else [high, high, middle, high, low, middle]
    one = jnp.ones_like(norm).astype(bf16)
    norms = list(split_three(norm))
    rows += [one, one, one] + norms if source else norms + [one, one, one]
    return [row.astype(f32) for row in rows]


def stage_coords(coords, origin, source, out_ref, base):
    leaves, panels = coords[0].shape
    rows = pieces_of([c - o for c, o in zip(coords, origin)], source)
    zeros = jnp.zeros((depth - len(rows), panels), f32)
    for leaf in range(leaves):
        group = [row[leaf : leaf + 1] for row in rows] + [zeros]
        out_ref[base + leaf] = jnp.concatenate(group, axis=0).astype(bf16)


def coef_place(leaf, scen, rank, panels, first_row):
    per_row = panels // rank
    row = first_row + leaf // per_row * scen
    lane = leaf % per_row * rank
    return slice(row, row + scen), slice(lane, lane + rank)


def prep_kernel(
    charges_ref, coords_ref, areas_ref, col_ref, up_ref, near_ref, far_ref,
    pack_ref, node_ref, pairs_ref, target_ref, source_ref, charge_ref,
):
    leaves, scen, panels = charges_ref.shape
    rank = col_ref.shape[1]
    coord_row = leaves * scen
    coef_row = coord_row + leaves * dims

    node = jnp.zeros((scen, rank), f32)
    for leaf in range(leaves):
        charge = charges_ref[leaf]
        weighted = charge * (areas_ref[leaf : leaf + 1] * inv_four_pi)
        pack_ref[leaf * scen : (leaf + 1) * scen] = weighted
        high, low = split(weighted)
        charge_ref[leaf, :scen] = high
        charge_ref[leaf, scen:] = low
        coef = dot_split(charge, col_ref[leaf], 1)
        pack_ref[coef_place(leaf, scen, rank, panels, coef_row)] = coef
        node = node + dot_split(coef, up_ref[leaf], 1)
    node_ref[...] = node
    coords = [coords_ref[axis] for axis in range(dims)]
    origin = [jnp.mean(c) for c in coords]
    for axis in range(dims):
        pack_ref[coord_row + axis * leaves : coord_row + (axis + 1) * leaves] = coords[axis]
    stage_coords(coords, origin, False, target_ref, 0)
    stage_coords(coords, origin, True, source_ref, 0)

    slots = near_ref.shape[1]
    count = leaves * slots
    near = near_ref[...]
    base = near[0:1, 0:1] - leaves

    def flat(table):
        n = table.shape[1]
        spread = jnp.where(
            lax.rem(lax.broadcasted_iota(jnp.int32, (n, count), 1), n)
            == lax.broadcasted_iota(jnp.int32, (n, count), 0), 1.0, 0.0
        )
        wide = jnp.dot(table.astype(f32).astype(bf16), spread.astype(bf16), preferred_element_type=f32)
        mine = lax.broadcasted_iota(jnp.int32, (leaves, count), 1) // n == lax.broadcasted_iota(
            jnp.int32, (leaves, count), 0
        )
        return jnp.sum(jnp.where(mine, wide, 0.0), axis=0, keepdims=True)

    source = flat(near - base)
    partners = far_ref.shape[0]
    far_slots = far_ref[...].astype(jnp.int32) - jnp.broadcast_to(base, far_ref.shape)
    own_rows = jnp.broadcast_to(
        jnp.where((source >= leaves) & (source < 2 * leaves), 1.0, 0.0), (8, count)
    )
    rows = lax.broadcasted_iota(jnp.int32, (count, count), 0)
    cols = lax.broadcasted_iota(jnp.int32, (count, count), 1)
    earlier = jnp.where(rows < cols, 1.0, 0.0).astype(bf16)
    own_before = jnp.dot(own_rows.astype(bf16), earlier, preferred_element_type=f32)
    total = jnp.sum(own_rows, axis=1, keepdims=True)
    index = lax.broadcasted_iota(jnp.int32, (8, count), 1)
    spot = jnp.where(own_rows > 0.0, own_before, total + index.astype(f32) - own_before)
    chosen = jnp.where(rows == spot[:1].astype(jnp.int32), 1.0, 0.0).astype(bf16)
    kind = lax.broadcasted_iota(jnp.int32, (8, count), 0)
    values = jnp.where(kind == 0, (index // slots).astype(f32), jnp.broadcast_to(source, (8, count)))
    values = lax.dot_general(
        values.astype(bf16), chosen, (((1,), (1,)), ((), ())), preferred_element_type=f32
    )
    pairs_ref[...] = jnp.where(kind == 2, total, values).astype(jnp.int32)
    pairs_ref[4 : 4 + partners, :leaves] = far_slots


def stage_kernel(
    pairs_ref, own_ref, below_ref, above_ref, own_source_ref, own_charge_ref, coupling_ref,
    source_ref, charge_ref, local_ref, coef_ref,
):
    leaves, scen = local_ref.shape[:2]
    rank = local_ref.shape[2]
    panels = own_ref.shape[1]
    coord_row = leaves * scen
    coef_row = coord_row + leaves * dims

    def coords_of(pack_ref):
        return [
            pack_ref[coord_row + axis * leaves : coord_row + (axis + 1) * leaves]
            for axis in range(dims)
        ]

    origin = [jnp.mean(c) for c in coords_of(own_ref)]
    source_ref[leaves : 2 * leaves] = own_source_ref[...]
    charge_ref[leaves : 2 * leaves] = own_charge_ref[...]
    for place, pack_ref in enumerate((below_ref, own_ref, above_ref)):
        if place != 1:
            stage_coords(coords_of(pack_ref), origin, True, source_ref, place * leaves)
        for leaf in range(leaves):
            slot = place * leaves + leaf
            if place != 1:
                high, low = split(pack_ref[leaf * scen : (leaf + 1) * scen])
                charge_ref[slot, :scen] = high
                charge_ref[slot, scen:] = low
            coef_ref[slot] = pack_ref[coef_place(leaf, scen, rank, panels, coef_row)]
    for leaf in range(leaves):
        total = jnp.zeros((scen, rank), f32)
        for partner in range(coupling_ref.shape[1]):
            total = total + dot_split(coef_ref[pairs_ref[4 + partner, leaf]], coupling_ref[leaf, partner], 1)
        local_ref[leaf] = total


def near_kernel(halo, part, parts, pairs_ref, target_ref, source_ref, charge_ref, *refs):
    out_ref, high_ref, low_ref = refs[-3:]
    start_ref = refs[0] if len(refs) > 3 else None
    leaves, scen, panels = out_ref.shape
    shift_down = 0 if halo else leaves
    if start_ref is None:
        out_ref[...] = jnp.zeros_like(out_ref)
    else:
        out_ref[...] = start_ref[...]
    count = pairs_ref.shape[1]
    own_chunks = pairs_ref[2, 0] // chunk
    first, size = (own_chunks, count // chunk - own_chunks) if halo else (0, own_chunks)
    begin = first + size * part // parts
    end = first + size * (part + 1) // parts

    def generate(pair, slot):
        pair = jnp.minimum(pair, end * chunk - 1)
        square = lax.dot_general(
            source_ref[jnp.maximum(pairs_ref[1, pair] - shift_down, 0)],
            target_ref[pairs_ref[0, pair]],
            (((0,), (0,)), ((), ())),
            preferred_element_type=f32,
        )
        high, low = split(lax.rsqrt(square))
        high_ref[slot] = high
        low_ref[slot] = low

    def apply(pair, slot):
        target = pairs_ref[0, pair]
        charge = charge_ref[pairs_ref[1, pair] - shift_down]
        first = jnp.dot(charge, high_ref[slot], preferred_element_type=f32)
        second = jnp.dot(charge[:scen], low_ref[slot], preferred_element_type=f32)
        out_ref[target] += first[:scen] + first[scen:] + second

    @pl.when(begin < end)
    def _():
        for step in range(ahead):
            generate(begin * chunk + step, step)

        def body(step, carry):
            for half in range(2):
                base = step * chunk + half * ahead
                for lane in range(ahead):
                    generate(base + ahead + lane, (1 - half) * ahead + lane)
                    apply(base + lane, half * ahead + lane)
            return carry

        lax.fori_loop(begin, end, body, 0)


def far_kernel(
    place_ref, local_ref, siblings_ref, roots_ref, down_ref, row_ref, down_transfer_ref, sibling_ref,
    branch_ref, near_ref, out_ref,
):
    leaves, scen, panels = near_ref.shape
    rank = down_ref.shape[1]
    levels = down_transfer_ref.shape[1]
    cluster_idx = place_ref[0]
    downward = jnp.zeros((scen, rank), f32)
    for other in range(roots_ref.shape[0]):
        downward = downward + dot_split(roots_ref[other], branch_ref[0, other], 1)
    for level in reversed(range(levels)):
        parity = (cluster_idx >> level) & 1
        downward = dot_split(siblings_ref[level], sibling_ref[0, level, parity], 1) + dot_split(
            downward, down_transfer_ref[0, level, parity], 1
        )
    for leaf in range(leaves):
        total = local_ref[leaf] + dot_split(downward, down_ref[leaf], 1)
        out_ref[leaf] = near_ref[leaf] + dot_split(total, row_ref[leaf], 0)


def shift(block, axis, step):
    count = lax.axis_size(axis)
    return lax.ppermute(
        block, axis, [(i, i + step) for i in range(count) if 0 <= i + step < count]
    )


def on_device(
    charges, coords, areas, col_basis, row_basis, leaf_up, leaf_down, leaf_coupling,
    up_transfer, down_transfer, sibling_coupling, branch_coupling, near_list, far_list,
):
    leaves, scen, panels = charges.shape
    rank = col_basis.shape[1]
    clusters, branches = lax.axis_size("cluster"), lax.axis_size("branch")
    levels = up_transfer.shape[1]
    cluster_idx = lax.axis_index("cluster")
    count = near_list.size
    pack_rows = leaves * scen + leaves * dims + leaves * scen * rank // panels

    def stages(places):
        return (
            jax.ShapeDtypeStruct((places * leaves, depth, panels), bf16),
            jax.ShapeDtypeStruct((places * leaves, 2 * scen, panels), bf16),
        )

    pack, node, pairs, target, own_source, own_charge = pl.pallas_call(
        prep_kernel,
        out_shape=(
            jax.ShapeDtypeStruct((pack_rows, panels), f32),
            jax.ShapeDtypeStruct((scen, rank), f32),
            jax.ShapeDtypeStruct((8, count), jnp.int32),
            jax.ShapeDtypeStruct((leaves, depth, panels), bf16),
            *stages(1),
        ),
        in_specs=[vmem] * 7,
        out_specs=(vmem,) * 6,
        compiler_params=params,
        name="prep",
    )(charges, coords.transpose(1, 0, 2), areas, col_basis, leaf_up, near_list, far_list.T)

    below = shift(pack, "cluster", 1)
    above = shift(pack, "cluster", -1)
    out = jax.ShapeDtypeStruct((leaves, scen, panels), f32)
    entries = count * panels * panels

    def near(halo, part, parts, source, charge, start):
        args = [pairs, target, source, charge] + ([] if start is None else [start])
        return pl.pallas_call(
            functools.partial(near_kernel, halo, part, parts),
            out_shape=out,
            in_specs=[smem] + [vmem] * (len(args) - 1),
            out_specs=vmem,
            scratch_shapes=[pltpu.VMEM((chunk, panels, panels), bf16)] * 2,
            compiler_params=params,
            cost_estimate=pl.CostEstimate(
                flops=entries * 20, bytes_accessed=2**20, transcendentals=entries // 4
            ),
            name="near_halo" if halo else "near_own",
        )(*args)

    def exchange(values, level):
        return lax.ppermute(values, "cluster", [(i, i ^ 1 << level) for i in range(clusters)])

    def combine(values, sibling, level):
        parity = cluster_idx >> level & 1
        left = jnp.where(parity == 0, values, sibling)
        right = jnp.where(parity == 0, sibling, values)
        both = [
            lax.dot_general(side, up_transfer[0, level, i], (((1,), (1,)), ((), ())), precision=lax.Precision.HIGHEST)
            for i, side in enumerate((left, right))
        ]
        return both[0] + both[1]

    tie = lax.optimization_barrier
    current, siblings, done = node, [], 0

    def climb(current, work):
        level = len(siblings)
        if level < levels:
            sibling = exchange(current, level)
            work, sibling = tie((work(), sibling))
            siblings.append(sibling)
            return combine(current, sibling, level), work
        return current, work()

    current, near_part = climb(current, lambda: near(False, 0, 2, own_source, own_charge, None))
    current, near_part = climb(current, lambda: near(False, 1, 2, own_source, own_charge, near_part))

    def stage():
        return pl.pallas_call(
            stage_kernel,
            out_shape=(*stages(3), jax.ShapeDtypeStruct((leaves, scen, rank), f32)),
            in_specs=[smem] + [vmem] * 6,
            out_specs=(vmem,) * 3,
            scratch_shapes=[pltpu.VMEM((3 * leaves, scen, rank), f32)],
            compiler_params=params,
            name="stage",
        )(pairs, pack, below, above, own_source, own_charge, leaf_coupling)

    current, (source, charge, local) = climb(current, stage)
    current, near_part = climb(current, lambda: near(True, 0, 2, source, charge, near_part))
    while len(siblings) < levels:
        current, _ = climb(current, lambda: jnp.zeros(()))
    roots = [
        lax.ppermute(current, "branch", [((i + 1 + other) % branches, i) for i in range(branches)])
        for other in range(branches - 1)
    ]
    near_part, roots = tie((near(True, 1, 2, source, charge, near_part), roots))
    return pl.pallas_call(
        far_kernel,
        out_shape=out,
        in_specs=[smem] + [vmem] * 9,
        out_specs=vmem,
        compiler_params=params,
        name="far",
    )(
        cluster_idx.reshape(1).astype(jnp.int32), local, jnp.stack(siblings), jnp.stack(roots),
        leaf_down, row_basis, down_transfer, sibling_coupling, branch_coupling, near_part,
    )


def solution(mesh):
    leaf3 = P(("branch", "cluster"), None, None)
    leaf2 = P(("branch", "cluster"), None)
    leaf4 = P(("branch", "cluster"), None, None, None)
    tree = P("branch", None, None, None, None)
    in_specs = (
        leaf3, leaf3, leaf2, leaf3, leaf3, leaf3, leaf3, leaf4,
        tree, tree, tree, P("branch", None, None, None), leaf2, leaf2,
    )
    return jax.shard_map(
        on_device, mesh=mesh, in_specs=in_specs, out_specs=leaf3, check_vma=False
    )
```

time: 186 us -> 67.4 us (0.36)
  the two profiles are of different devices: /device:TPU:0 before, /device:TPU:5 now
where the time goes in v1:
time: 67.4 us; the launch traced here: 66.5 us
  Pallas kernels  35.4 us (53%)
  starting transfers between devices  15 us (22%)
  local copies, waits for them, and re-layouts  11.5 us (17%)
  matrix products  4.3 us (6%)
    pallas_call x4, Pallas kernels, near(): pl.pallas_call(functools.partial(near_kernel, halo, part, parts), out_sha...  28.1 us
    unnamed x48, local copies, waits for them, and re-layouts  11.5 us
    ppermute x4, starting transfers between devices, exchange(): lax.ppermute(values, 'cluster', [(i, i ^ 1 << level) for i in range(clust...  8.88 us
    ppermute x2, starting transfers between devices, shift(): lax.ppermute(block, axis, [(i, i + step) for i in range(count) if 0 <= i...  5.64 us
    dot_general x8, matrix products, combine(): lax.dot_general(side, up_transfer[0, level, i], (((1,), (1,)), ((), ())),...  4.3 us
    pallas_call x1, Pallas kernels, on_device(): pl.pallas_call(far_kernel, out_shape=out, in_specs=[smem] + [vmem] * 9, o...  3.8 us
    pallas_call x1, Pallas kernels, stage(): pl.pallas_call(stage_kernel, out_shape=(*stages(3), jax.ShapeDtypeStruct(...  2.25 us
  transfers between devices with their start and end apart: 7, of which 0 were waited for; matrix products, arithmetic and copies ran while one was open for 6% of the time, Pallas kernels for 46%

profile of v1, /device:TPU:5, one launch (start us, length us, event | category | flops | bytes accessed | tf_op | source)
XLA Modules:
  0.0 66.5 jit_solution(3304544599986114939)
XLA Ops:
  0.0 1.2 %copy-done.2 = f32[16,64,256]{2,1,0:T(8,128)S(1)} copy-done((f32[16,64,256]{2,1,0:T(8,128)S(1)}, f32[16,64,256]{2,1,0:T(8,128)}, u32[]{:S(2)}) %copy-start.2) | copy-done | bytes 1048600
  1.2 1.0 %copy-done.3 = f32[16,64,64]{2,1,0:T(8,128)S(1)} copy-done((f32[16,64,64]{2,1,0:T(8,128)S(1)}, f32[16,64,64]{2,1,0:T(8,128)}, u32[]{:S(2)}) %copy-start.3) | copy-done | bytes 262168
  2.3 0.9 %copy-done.10 = f32[16,16,256]{2,1,0:T(8,128)S(1)} copy-done((f32[16,16,256]{2,1,0:T(8,128)S(1)}, f32[16,16,256]{2,1,0:T(8,128)}, u32[]{:S(2)}) %copy-start.10) | copy-done | bytes 262168
  3.2 0.8 %copy-done.11 = f32[16,3,256]{2,0,1:T(8,128)S(1)} copy-done((f32[16,3,256]{2,0,1:T(8,128)S(1)}, f32[16,3,256]{2,0,1:T(8,128)}, u32[]{:S(2)}) %copy-start.11) | copy-done | bytes 49176
  4.0 0.7 %copy-done.13 = f32[16,256]{1,0:T(8,128)S(1)} copy-done((f32[16,256]{1,0:T(8,128)S(1)}, f32[16,256]{1,0:T(8,128)}, u32[]{:S(2)}) %copy-start.13) | copy-done | bytes 16408
  4.7 0.7 %copy-done.14 = s32[16,16]{1,0:T(8,128)S(1)} copy-done((s32[16,16]{1,0:T(8,128)S(1)}, s32[16,16]{1,0:T(8,128)}, u32[]{:S(2)}) %copy-start.14) | copy-done | bytes 1048
  5.4 0.7 %copy-done.15 = s32[16,4]{0,1:T(4,128)S(1)} copy-done((s32[16,4]{0,1:T(4,128)S(1)}, s32[16,4]{0,1:T(4,128)}, u32[]{:S(2)}) %copy-start.15) | copy-done | bytes 280
  6.1 1.3 %prep.1 = (f32[368,256]{1,0:T(8,128)S(1)}, f32[16,64]{1,0:T(8,128)S(1)}, s32[8,256]{1,0:T(8,128)S(1)}, bf16[16,32,256]{2,1,0:T(8,128)(2,1)S(1)}, bf16[16,32,256]...) custom-call(f32[16,16,256]{2,1,0:T(8,128)S(1)} %copy-done.10, f32[3,16,256]{2,1,0:T(8,128)S(1)} %bitcast.32, ...), custom_call_target="tpu_custom_call" | custom-call | tf_op jit(solution)/shard_map/prep/pallas_call | solution.py:278
  7.4 3.7 %collective-permute-start = (f32[368,256]{1,0:T(8,128)S(1)}, f32[368,256]{1,0:T(8,128)S(1)}, u32[]{:S(2)}, u32[]{:S(2)}) collective-permute-start(f32[368,256]{1,0:T(8,128)S(1)} %get-tuple-element.27.own_ref), channel_id=1, source_target_pairs={{0,1},{1,2},{2,3},{3,4},{4,5},{5,6},{6,7},{7,8},{8,9},{9,10},{10,1... | collective-permute-start | bytes 1130504 | tf_op jit(solution)/shard_map/ppermute | solution.py:255
  11.1 1.9 %collective-permute-start.1 = (f32[368,256]{1,0:T(8,128)S(1)}, f32[368,256]{1,0:T(8,128)S(1)}, u32[]{:S(2)}, u32[]{:S(2)}) collective-permute-start(f32[368,256]{1,0:T(8,128)S(1)} %get-tuple-element.27.own_ref), channel_id=1, source_target_pairs={{1,0},{2,1},{3,2},{4,3},{5,4},{6,5},{7,6},{8,7},{9,8},{10,9},{11,1... | collective-permute-start | bytes 1130504 | tf_op jit(solution)/shard_map/ppermute | solution.py:255
  13.0 0.7 %collective-permute-start.2 = (f32[16,64]{1,0:T(8,128)S(1)}, f32[16,64]{1,0:T(8,128)S(1)}, u32[]{:S(2)}, u32[]{:S(2)}) collective-permute-start(f32[16,64]{1,0:T(8,128)S(1)} %get-tuple-element.33), channel_id=1, source_target_pairs={{0,1},{1,0},{2,3},{3,2},{4,5},{5,4},{6,7},{7,6},{8,9},{9,8},{10,11... | collective-permute-start | bytes 12296 | tf_op jit(solution)/shard_map/ppermute | solution.py:314
  13.7 4.8 %near_own.2.refs_0_ = f32[16,16,256]{2,1,0:T(8,128)S(1)} custom-call(s32[8,256]{1,0:T(8,128)S(1)} %get-tuple-element.26.pairs_ref, bf16[16,32,256]{2,1,0:T(8,128)(2,1)S(1)} %get-tuple-element.34.target_ref, bf16[16,32,256]{2,1,0:T(8,128)(2,1)S(1)} %get-tuple-element.28.own_source_ref.source_ref, ...), custom_call_target="tpu_custom_call" | custom-call | flops 335544320 | bytes 1048576 | tf_op jit(solution)/shard_map/near_own/pallas_call | solution.py:300
  18.6 0.7 %copy-done.21 = f32[16,16,256]{2,1,0:T(8,128)} copy-done((f32[16,16,256]{2,1,0:T(8,128)}, f32[16,16,256]{2,1,0:T(8,128)S(1)}, u32[]{:S(2)}) %copy-start.21) | copy-done | bytes 262168
  19.3 0.9 %fusion.9 = f32[16,64]{1,0:T(8,128)S(1)} fusion(f32[1,4,2,64,64]{4,3,2,1,0:T(8,128)} %param.22, f32[16,64]{1,0:T(8,128)S(1)} %collective-permute-done.2, f32[16,64]{1,0:T(8,128)S(1)} %get-tuple-element.33, pred[]{:T(512)S(6)} %eq.17), kind=kOutput, calls=%fused_computation.14 | convolution fusion | flops 787456 | bytes 45057 | tf_op jit(solution)/shard_map/dot_general | solution.py:321
  20.2 0.9 %convolution_add_fusion.3 = f32[16,64]{1,0:T(8,128)S(1)} fusion(f32[16,64]{1,0:T(8,128)S(1)} %fusion.9, f32[1,4,2,64,64]{4,3,2,1,0:T(8,128)} %param.22, f32[16,64]{1,0:T(8,128)S(1)} %get-tuple-element.33, f32[16,64]{1,0:T(8,128)S(1)} %collective-permute-done.2, pred[]{:T(512)S(6)} %eq.17), kind=kOutput, calls=%fused_computation.3 | convolution fusion | flops 788480 | bytes 49153 | tf_op jit(solution)/shard_map/dot_general | solution.py:321
  21.2 1.1 %copy-done.6 = bf16[16,32,256]{2,1,0:T(8,128)(2,1)S(1)} copy-done((bf16[16,32,256]{2,1,0:T(8,128)(2,1)S(1)}, bf16[16,32,256]{2,1,0:T(8,128)(2,1)}, u32[]{:S(2)}) %copy-start.6) | copy-done | bytes 262168
  22.3 0.9 %copy-done.17 = bf16[16,32,256]{2,1,0:T(8,128)(2,1)S(1)} copy-done((bf16[16,32,256]{2,1,0:T(8,128)(2,1)S(1)}, bf16[16,32,256]{2,1,0:T(8,128)(2,1)}, u32[]{:S(2)}) %copy-start.17) | copy-done | bytes 262168
  23.2 0.9 %copy-done.22 = f32[16,16,256]{2,1,0:T(8,128)S(1)} copy-done((f32[16,16,256]{2,1,0:T(8,128)S(1)}, f32[16,16,256]{2,1,0:T(8,128)}, u32[]{:S(2)}) %copy-start.22) | copy-done | bytes 262168
  24.2 5.5 %near_own.3.refs_0_ = f32[16,16,256]{2,1,0:T(8,128)S(1)} custom-call(s32[8,256]{1,0:T(8,128)S(1)} %get-tuple-element.26.pairs_ref, bf16[16,32,256]{2,1,0:T(8,128)(2,1)S(1)} %copy-done.17, bf16[16,32,256]{2,1,0:T(8,128)(2,1)S(1)} %get-tuple-element.28.own_source_ref.source_ref, bf16[16,32,256]{2,1,0:T(8,128)(2,1)S(1)} %copy-done.6, f32[16,16,256]{2,1,0:T(8,128)S(1)} %copy-done.22), custom_call_target="tpu_custom_call" | custom-call | flops 335544320 | bytes 1048576 | tf_op jit(solution)/shard_map/near_own/pallas_call | solution.py:300
  29.8 0.7 %copy-done.19 = f32[16,16,256]{2,1,0:T(8,128)} copy-done((f32[16,16,256]{2,1,0:T(8,128)}, f32[16,16,256]{2,1,0:T(8,128)S(1)}, u32[]{:S(2)}) %copy-start.19) | copy-done | bytes 262168
  30.5 0.9 %fusion.6 = f32[16,64]{1,0:T(8,128)S(1)} fusion(f32[1,4,2,64,64]{4,3,2,1,0:T(8,128)} %param.22, f32[16,64]{1,0:T(8,128)S(1)} %collective-permute-done.3, f32[16,64]{1,0:T(8,128)S(1)} %convolution_add_fusion.3, pred[]{:T(512)S(6)} %eq.16), kind=kOutput, calls=%fused_computation.11 | convolution fusion | flops 787456 | bytes 45057 | tf_op jit(solution)/shard_map/dot_general | solution.py:321
  31.4 0.9 %convolution_add_fusion.2 = f32[16,64]{1,0:T(8,128)S(1)} fusion(f32[16,64]{1,0:T(8,128)S(1)} %fusion.6, f32[1,4,2,64,64]{4,3,2,1,0:T(8,128)} %param.22, f32[16,64]{1,0:T(8,128)S(1)} %convolution_add_fusion.3, f32[16,64]{1,0:T(8,128)S(1)} %collective-permute-done.3, pred[]{:T(512)S(6)} %eq.16), kind=kOutput, calls=%fused_computation.2 | convolution fusion | flops 788480 | bytes 49153 | tf_op jit(solution)/shard_map/dot_general | solution.py:321
  32.3 2.3 %collective-permute-start.4 = (f32[16,64]{1,0:T(8,128)S(1)}, f32[16,64]{1,0:T(8,128)S(1)}, u32[]{:S(2)}, u32[]{:S(2)}) collective-permute-start(f32[16,64]{1,0:T(8,128)S(1)} %convolution_add_fusion.2), channel_id=1, source_target_pairs={{0,4},{1,5},{2,6},{3,7},{4,0},{5,1},{6,2},{7,3},{8,12},{9,13},{10,... | collective-permute-start | bytes 12296 | tf_op jit(solution)/shard_map/ppermute | solution.py:314
  34.6 0.9 %copy-done.7 = bf16[16,32,256]{2,1,0:T(8,128)(2,1)S(1)} copy-done((bf16[16,32,256]{2,1,0:T(8,128)(2,1)S(1)}, bf16[16,32,256]{2,1,0:T(8,128)(2,1)}, u32[]{:S(2)}) %copy-start.7) | copy-done | bytes 262168
  35.6 2.3 %stage.1 = (bf16[48,32,256]{2,1,0:T(8,128)(2,1)S(1)}, bf16[48,32,256]{2,1,0:T(8,128)(2,1)S(1)}, f32[16,16,64]{2,1,0:T(8,128)S(1)}) custom-call(s32[8,256]{1,0:T(8,128)S(1)} %get-tuple-element.26.pairs_ref, f32[368,256]{1,0:T(8,128)S(1)} %get-tuple-element.27.own_ref, f32[368,256]{1,0:T(8,128)S(1)} %collective-permute-done.below_ref, ...), custom_call_target="tpu_custom_call" | custom-call | tf_op jit(solution)/shard_map/stage/pallas_call | solution.py:342
  38.0 0.2 convolution_add_fusion.1
  38.2 5.8 %collective-permute-start.5 = (f32[16,64]{1,0:T(8,128)S(1)}, f32[16,64]{1,0:T(8,128)S(1)}, u32[]{:S(2)}, u32[]{:S(2)}) collective-permute-start(f32[16,64]{1,0:T(8,128)S(1)} %convolution_add_fusion.1), channel_id=1, source_target_pairs={{0,8},{1,9},{2,10},{3,11},{4,12},{5,13},{6,14},{7,15},{8,0},{9,1},... | collective-permute-start | bytes 12296 | tf_op jit(solution)/shard_map/ppermute | solution.py:314
  44.0 8.5 %near_halo.2.refs_0_ = f32[16,16,256]{2,1,0:T(8,128)S(1)} custom-call(s32[8,256]{1,0:T(8,128)S(1)} %get-tuple-element.26.pairs_ref, bf16[16,32,256]{2,1,0:T(8,128)(2,1)S(1)} %copy-done.18, bf16[48,32,256]{2,1,0:T(8,128)(2,1)S(1)} %get-tuple-element.40.source_ref, bf16[48,32,256]{2,1,0:T(8,128)(2,1)S(1)} %get-tuple-element.41.charge_ref, ...), custom_call_target="tpu_custom_call" | custom-call | flops 335544320 | bytes 1048576 | tf_op jit(solution)/shard_map/near_halo/pallas_call | solution.py:300
  52.7 0.2 convolution_add_fusion
  52.8 0.5 collective-permute-start.6
  53.4 9.3 %near_halo.3.near_ref = f32[16,16,256]{2,1,0:T(8,128)S(1)} custom-call(s32[8,256]{1,0:T(8,128)S(1)} %get-tuple-element.26.pairs_ref, bf16[16,32,256]{2,1,0:T(8,128)(2,1)S(1)} %copy-done.18, bf16[48,32,256]{2,1,0:T(8,128)(2,1)S(1)} %get-tuple-element.40.source_ref, bf16[48,32,256]{2,1,0:T(8,128)(2,1)S(1)} %get-tuple-element.41.charge_ref, ...), custom_call_target="tpu_custom_call" | custom-call | flops 335544320 | bytes 1048576 | tf_op jit(solution)/shard_map/near_halo/pallas_call | solution.py:300
  62.7 3.8 %far.1 = f32[16,16,256]{2,1,0:T(8,128)} custom-call(s32[1]{0:T(128)} %bitcast.place_ref, f32[16,16,64]{2,1,0:T(8,128)S(1)} %get-tuple-element.38.local_ref, f32[4,16,64]{2,1,0:T(8,128)S(1)} %pad_maximum_fusion.siblings_ref, f32[1,16,64]{2,1,0:T(8,128)S(1)} %bitcast.33, f32[16,64,64]{2,1,0:T(8,128)S(1)} %copy-done.4, f32[16,64,256]{2,1,0:T(8,128)S(1)} %copy-done.1, ...), custom_call_target="tpu_custom_call" | custom-call | tf_op jit(solution)/shard_map/far/pallas_call | solution.py:361
  (46 shorter events, 0.5 us)
Async XLA Ops:
  0.0 1.2 %copy-start.2 = (f32[16,64,256]{2,1,0:T(8,128)S(1)}, f32[16,64,256]{2,1,0:T(8,128)}, u32[]{:S(2)}) copy-start(f32[16,64,256]{2,1,0:T(8,128)} %col_ref.1) | copy-start | bytes 3145732
  1.2 1.0 %copy-start.3 = (f32[16,64,64]{2,1,0:T(8,128)S(1)}, f32[16,64,64]{2,1,0:T(8,128)}, u32[]{:S(2)}) copy-start(f32[16,64,64]{2,1,0:T(8,128)} %up_ref.1) | copy-start | bytes 786436
  2.3 0.9 %copy-start.10 = (f32[16,16,256]{2,1,0:T(8,128)S(1)}, f32[16,16,256]{2,1,0:T(8,128)}, u32[]{:S(2)}) copy-start(f32[16,16,256]{2,1,0:T(8,128)} %charges_ref.1) | copy-start | bytes 786436
  3.2 0.8 %copy-start.11 = (f32[16,3,256]{2,0,1:T(8,128)S(1)}, f32[16,3,256]{2,0,1:T(8,128)}, u32[]{:S(2)}) copy-start(f32[16,3,256]{2,0,1:T(8,128)} %param.15) | copy-start | bytes 147460
  4.0 0.7 %copy-start.13 = (f32[16,256]{1,0:T(8,128)S(1)}, f32[16,256]{1,0:T(8,128)}, u32[]{:S(2)}) copy-start(f32[16,256]{1,0:T(8,128)} %areas_ref.1) | copy-start | bytes 49156
  4.7 0.7 %copy-start.14 = (s32[16,16]{1,0:T(8,128)S(1)}, s32[16,16]{1,0:T(8,128)}, u32[]{:S(2)}) copy-start(s32[16,16]{1,0:T(8,128)} %near_ref.1) | copy-start | bytes 3076
  5.4 0.7 %copy-start.15 = (s32[16,4]{0,1:T(4,128)S(1)}, s32[16,4]{0,1:T(4,128)}, u32[]{:S(2)}) copy-start(s32[16,4]{0,1:T(4,128)} %param.27) | copy-start | bytes 772
  7.4 11.2 %copy-start.5 = (bf16[16,32,256]{2,1,0:T(8,128)(2,1)}, bf16[16,32,256]{2,1,0:T(8,128)(2,1)S(1)}, u32[]{:S(2)}) copy-start(bf16[16,32,256]{2,1,0:T(8,128)(2,1)S(1)} %get-tuple-element.29.own_charge_ref.charge_ref) | copy-start | bytes 786436
  7.4 11.2 %copy-start.16 = (bf16[16,32,256]{2,1,0:T(8,128)(2,1)}, bf16[16,32,256]{2,1,0:T(8,128)(2,1)S(1)}, u32[]{:S(2)}) copy-start(bf16[16,32,256]{2,1,0:T(8,128)(2,1)S(1)} %get-tuple-element.34.target_ref) | copy-start | bytes 786436
  7.4 27.2 %collective-permute-start = (f32[368,256]{1,0:T(8,128)S(1)}, f32[368,256]{1,0:T(8,128)S(1)}, u32[]{:S(2)}, u32[]{:S(2)}) collective-permute-start(f32[368,256]{1,0:T(8,128)S(1)} %get-tuple-element.27.own_ref), channel_id=1, source_target_pairs={{0,1},{1,2},{2,3},{3,4},{4,5},{5,6},{6,7},{7,8},{8,9},{9,10},{10,1... | collective-permute-start | bytes 1130504 | tf_op jit(solution)/shard_map/ppermute | solution.py:255
  11.1 23.5 %collective-permute-start.1 = (f32[368,256]{1,0:T(8,128)S(1)}, f32[368,256]{1,0:T(8,128)S(1)}, u32[]{:S(2)}, u32[]{:S(2)}) collective-permute-start(f32[368,256]{1,0:T(8,128)S(1)} %get-tuple-element.27.own_ref), channel_id=1, source_target_pairs={{1,0},{2,1},{3,2},{4,3},{5,4},{6,5},{7,6},{8,7},{9,8},{10,9},{11,1... | collective-permute-start | bytes 1130504 | tf_op jit(solution)/shard_map/ppermute | solution.py:255
  13.0 6.2 %collective-permute-start.2 = (f32[16,64]{1,0:T(8,128)S(1)}, f32[16,64]{1,0:T(8,128)S(1)}, u32[]{:S(2)}, u32[]{:S(2)}) collective-permute-start(f32[16,64]{1,0:T(8,128)S(1)} %get-tuple-element.33), channel_id=1, source_target_pairs={{0,1},{1,0},{2,3},{3,2},{4,5},{5,4},{6,7},{7,6},{8,9},{9,8},{10,11... | collective-permute-start | bytes 12296 | tf_op jit(solution)/shard_map/ppermute | solution.py:314
  18.5 0.7 %copy-start.21 = (f32[16,16,256]{2,1,0:T(8,128)}, f32[16,16,256]{2,1,0:T(8,128)S(1)}, u32[]{:S(2)}) copy-start(f32[16,16,256]{2,1,0:T(8,128)S(1)} %near_own.2.refs_0_) | copy-start | bytes 786436
  21.1 13.5 %copy-start = (f32[16,4,64,64]{3,2,1,0:T(8,128)S(1)}, f32[16,4,64,64]{3,2,1,0:T(8,128)}, u32[]{:S(2)}) copy-start(f32[16,4,64,64]{3,2,1,0:T(8,128)} %coupling_ref.1) | copy-start | bytes 3145732
  21.1 9.3 %collective-permute-start.3 = (f32[16,64]{1,0:T(8,128)S(1)}, f32[16,64]{1,0:T(8,128)S(1)}, u32[]{:S(2)}, u32[]{:S(2)}) collective-permute-start(f32[16,64]{1,0:T(8,128)S(1)} %convolution_add_fusion.3), channel_id=1, source_target_pairs={{0,2},{1,3},{2,0},{3,1},{4,6},{5,7},{6,4},{7,5},{8,10},{9,11},{10,... | collective-permute-start | bytes 12296 | tf_op jit(solution)/shard_map/ppermute | solution.py:314
  21.2 1.1 %copy-start.6 = (bf16[16,32,256]{2,1,0:T(8,128)(2,1)S(1)}, bf16[16,32,256]{2,1,0:T(8,128)(2,1)}, u32[]{:S(2)}) copy-start(bf16[16,32,256]{2,1,0:T(8,128)(2,1)} %copy-done.5) | copy-start | bytes 786436
  22.3 0.9 %copy-start.17 = (bf16[16,32,256]{2,1,0:T(8,128)(2,1)S(1)}, bf16[16,32,256]{2,1,0:T(8,128)(2,1)}, u32[]{:S(2)}) copy-start(bf16[16,32,256]{2,1,0:T(8,128)(2,1)} %copy-done.16) | copy-start | bytes 786436
  23.2 0.9 %copy-start.22 = (f32[16,16,256]{2,1,0:T(8,128)S(1)}, f32[16,16,256]{2,1,0:T(8,128)}, u32[]{:S(2)}) copy-start(f32[16,16,256]{2,1,0:T(8,128)} %copy-done.21) | copy-start | bytes 786436
  29.7 0.7 %copy-start.19 = (f32[16,16,256]{2,1,0:T(8,128)}, f32[16,16,256]{2,1,0:T(8,128)S(1)}, u32[]{:S(2)}) copy-start(f32[16,16,256]{2,1,0:T(8,128)S(1)} %near_own.3.refs_0_) | copy-start | bytes 786436
  32.3 5.5 %collective-permute-start.4 = (f32[16,64]{1,0:T(8,128)S(1)}, f32[16,64]{1,0:T(8,128)S(1)}, u32[]{:S(2)}, u32[]{:S(2)}) collective-permute-start(f32[16,64]{1,0:T(8,128)S(1)} %convolution_add_fusion.2), channel_id=1, source_target_pairs={{0,4},{1,5},{2,6},{3,7},{4,0},{5,1},{6,2},{7,3},{8,12},{9,13},{10,... | collective-permute-start | bytes 12296 | tf_op jit(solution)/shard_map/ppermute | solution.py:314
  34.6 1.0 %copy-start.7 = (bf16[16,32,256]{2,1,0:T(8,128)(2,1)S(1)}, bf16[16,32,256]{2,1,0:T(8,128)(2,1)}, u32[]{:S(2)}) copy-start(bf16[16,32,256]{2,1,0:T(8,128)(2,1)} %copy-done.5) | copy-start | bytes 786436
  35.6 2.3 %copy-start.23 = (f32[1,4,2,64,64]{4,3,2,1,0:T(8,128)S(1)}, f32[1,4,2,64,64]{4,3,2,1,0:T(8,128)}, u32[]{:S(2)}) copy-start(f32[1,4,2,64,64]{4,3,2,1,0:T(8,128)} %param.22) | copy-start | bytes 393220
  35.6 8.4 %copy-start.18 = (bf16[16,32,256]{2,1,0:T(8,128)(2,1)S(1)}, bf16[16,32,256]{2,1,0:T(8,128)(2,1)}, u32[]{:S(2)}) copy-start(bf16[16,32,256]{2,1,0:T(8,128)(2,1)} %copy-done.16) | copy-start | bytes 786436
  35.6 8.4 %copy-start.20 = (f32[16,16,256]{2,1,0:T(8,128)S(1)}, f32[16,16,256]{2,1,0:T(8,128)}, u32[]{:S(2)}) copy-start(f32[16,16,256]{2,1,0:T(8,128)} %copy-done.19) | copy-start | bytes 786436
  38.2 14.4 %collective-permute-start.5 = (f32[16,64]{1,0:T(8,128)S(1)}, f32[16,64]{1,0:T(8,128)S(1)}, u32[]{:S(2)}, u32[]{:S(2)}) collective-permute-start(f32[16,64]{1,0:T(8,128)S(1)} %convolution_add_fusion.1), channel_id=1, source_target_pairs={{0,8},{1,9},{2,10},{3,11},{4,12},{5,13},{6,14},{7,15},{8,0},{9,1},... | collective-permute-start | bytes 12296 | tf_op jit(solution)/shard_map/ppermute | solution.py:314
  52.8 9.8 %collective-permute-start.6 = (f32[16,64]{1,0:T(8,128)S(1)}, f32[16,64]{1,0:T(8,128)S(1)}, u32[]{:S(2)}, u32[]{:S(2)}) collective-permute-start(f32[16,64]{1,0:T(8,128)S(1)} %convolution_add_fusion), channel_id=1, source_target_pairs={{16,0},{0,16},{17,1},{1,17},{18,2},{2,18},{19,3},{3,19},{20,4},{4,... | collective-permute-start | bytes 12296 | tf_op jit(solution)/shard_map/ppermute | solution.py:357
  53.4 9.3 %copy-start.1 = (f32[16,64,256]{2,1,0:T(8,128)S(1)}, f32[16,64,256]{2,1,0:T(8,128)}, u32[]{:S(2)}) copy-start(f32[16,64,256]{2,1,0:T(8,128)} %row_ref.1) | copy-start | bytes 3145732
  53.4 9.3 %copy-start.4 = (f32[16,64,64]{2,1,0:T(8,128)S(1)}, f32[16,64,64]{2,1,0:T(8,128)}, u32[]{:S(2)}) copy-start(f32[16,64,64]{2,1,0:T(8,128)} %down_ref.1) | copy-start | bytes 786436
  53.4 9.3 %copy-start.8 = (f32[1,4,2,64,64]{4,3,2,1,0:T(8,128)S(1)}, f32[1,4,2,64,64]{4,3,2,1,0:T(8,128)}, u32[]{:S(2)}) copy-start(f32[1,4,2,64,64]{4,3,2,1,0:T(8,128)} %down_transfer_ref.1) | copy-start | bytes 393220
  53.4 9.3 %copy-start.9 = (f32[1,4,2,64,64]{4,3,2,1,0:T(8,128)S(1)}, f32[1,4,2,64,64]{4,3,2,1,0:T(8,128)}, u32[]{:S(2)}) copy-start(f32[1,4,2,64,64]{4,3,2,1,0:T(8,128)} %sibling_ref.1) | copy-start | bytes 393220
  53.4 9.3 %copy-start.12 = (f32[1,1,64,64]{3,2,1,0:T(8,128)S(1)}, f32[1,1,64,64]{3,2,1,0:T(8,128)}, u32[]{:S(2)}) copy-start(f32[1,1,64,64]{3,2,1,0:T(8,128)} %branch_ref.1) | copy-start | bytes 49156

commit v2 on v1

v2 whole, which is shorter than its diff:
```python
import functools
import math

import jax
import jax.numpy as jnp
from jax import lax
from jax.experimental import pallas as pl
from jax.experimental.pallas import tpu as pltpu
from jax.sharding import PartitionSpec as P

f32, bf16 = jnp.float32, jnp.bfloat16
reg_square = 0.01
inv_four_pi = 0.25 / math.pi
dims = 3
ahead = 8
chunk = 2 * ahead
vmem = pl.BlockSpec(memory_space=pltpu.VMEM)
smem = pl.BlockSpec(memory_space=pltpu.SMEM)
params = pltpu.CompilerParams(vmem_limit_bytes=16 * 2**20)
large = pltpu.CompilerParams(vmem_limit_bytes=58 * 2**20)
depth = 32
fine, wide = jnp.float8_e4m3fn, jnp.float8_e5m2
entry_scale, fine_scale = 2.0**13, 2.0**15
own_steps = 5


def split(x):
    high = x.astype(bf16)
    return high, (x - high.astype(f32)).astype(bf16)


def split_three(x):
    high, rest = x.astype(bf16), None
    rest = x - high.astype(f32)
    middle = rest.astype(bf16)
    return high, middle, (rest - middle.astype(f32)).astype(bf16)


def dot_split(a, b, contract):
    rows = a.shape[0]
    a_high, a_low = split(a)
    b_high, b_low = split(b)
    numbers = (((1,), (contract,)), ((), ()))
    first = lax.dot_general(
        jnp.concatenate([a_high, a_low], axis=0), b_high, numbers, preferred_element_type=f32
    )
    second = lax.dot_general(a_high, b_low, numbers, preferred_element_type=f32)
    return first[:rows] + first[rows:] + second


def pieces_of(coords, source):
    coords = [c * (1.0 / entry_scale) for c in coords]
    norm = coords[0] * coords[0] + coords[1] * coords[1] + coords[2] * coords[2]
    if not source:
        norm = norm + reg_square / entry_scale**2
        coords = [-2.0 * c for c in coords]
    rows = []
    for c in coords:
        high, middle, low = split_three(c)
        rows += [high, middle, high, low, high, middle] if source else [high, high, middle, high, low, middle]
    one = jnp.ones_like(norm).astype(bf16)
    norms = list(split_three(norm))
    rows += [one, one, one] + norms if source else norms + [one, one, one]
    return [row.astype(f32) for row in rows]


def stage_coords(coords, origin, source, out_ref, base):
    leaves, panels = coords[0].shape
    rows = pieces_of([c - o for c, o in zip(coords, origin)], source)
    zeros = jnp.zeros((depth - len(rows), panels), f32)
    for leaf in range(leaves):
        group = [row[leaf : leaf + 1] for row in rows] + [zeros]
        group = jnp.concatenate(group, axis=0)
        out_ref[base + leaf] = (group.T if source else group).astype(bf16)


def stage_charge(weighted, charge_ref, tail_ref, slot):
    scen = weighted.shape[0]
    high, low = split(weighted * (1.0 / entry_scale))
    charge_ref[slot, :scen] = high
    charge_ref[slot, scen:] = low
    weighted = weighted * fine_scale
    high = weighted.astype(wide)
    low = (weighted - high.astype(f32)).astype(wide)
    tail_ref[slot] = jnp.concatenate([high.astype(f32), low.astype(f32)], axis=0).astype(wide)


def coef_place(leaf, scen, rank, panels, first_row):
    per_row = panels // rank
    row = first_row + leaf // per_row * scen
    lane = leaf % per_row * rank
    return slice(row, row + scen), slice(lane, lane + rank)


def prep_kernel(
    cluster_ref, charges_ref, coords_ref, areas_ref, col_ref, up_ref, transfer_ref, near_ref, far_ref,
    pack_ref, nodes_ref, pairs_ref, target_ref, source_ref, charge_ref, tail_ref,
):
    leaves, scen, panels = charges_ref.shape
    rank = col_ref.shape[1]
    coord_row = leaves * scen
    coef_row = coord_row + leaves * dims

    path = None
    for level in range(transfer_ref.shape[1]):
        matrix = transfer_ref[0, level, (cluster_ref[0] >> level) & 1]
        path = matrix if path is None else dot_split(matrix, path, 0)

    node = jnp.zeros((scen, rank), f32)
    for leaf in range(leaves):
        charge = charges_ref[leaf]
        weighted = charge * (areas_ref[leaf : leaf + 1] * inv_four_pi)
        pack_ref[leaf * scen : (leaf + 1) * scen] = weighted
        stage_charge(weighted, charge_ref, tail_ref, leaf)
        coef = dot_split(charge, col_ref[leaf], 1)
        pack_ref[coef_place(leaf, scen, rank, panels, coef_row)] = coef
        node = node + dot_split(coef, up_ref[leaf], 1)
    node = jnp.concatenate([node, dot_split(node, path, 1)], axis=1)
    for device in range(nodes_ref.shape[0] // scen):
        nodes_ref[device * scen : (device + 1) * scen] = node
    coords = [coords_ref[axis] for axis in range(dims)]
    origin = [jnp.mean(c) for c in coords]
    for axis in range(dims):
        pack_ref[coord_row + axis * leaves : coord_row + (axis + 1) * leaves] = coords[axis]
    stage_coords(coords, origin, False, target_ref, 0)
    stage_coords(coords, origin, True, source_ref, 0)

    slots = near_ref.shape[1]
    count = leaves * slots
    near = near_ref[...]
    base = near[0:1, 0:1] - leaves

    def flat(table):
        n = table.shape[1]
        spread = jnp.where(
            lax.rem(lax.broadcasted_iota(jnp.int32, (n, count), 1), n)
            == lax.broadcasted_iota(jnp.int32, (n, count), 0), 1.0, 0.0
        )
        wide = jnp.dot(table.astype(f32).astype(bf16), spread.astype(bf16), preferred_element_type=f32)
        mine = lax.broadcasted_iota(jnp.int32, (leaves, count), 1) // n == lax.broadcasted_iota(
            jnp.int32, (leaves, count), 0
        )
        return jnp.sum(jnp.where(mine, wide, 0.0), axis=0, keepdims=True)

    source = flat(near - base)
    partners = far_ref.shape[0]
    far_slots = far_ref[...].astype(jnp.int32) - jnp.broadcast_to(base, far_ref.shape)
    own_rows = jnp.broadcast_to(
        jnp.where((source >= leaves) & (source < 2 * leaves), 1.0, 0.0), (8, count)
    )
    rows = lax.broadcasted_iota(jnp.int32, (count, count), 0)
    cols = lax.broadcasted_iota(jnp.int32, (count, count), 1)
    earlier = jnp.where(rows < cols, 1.0, 0.0).astype(bf16)
    own_before = jnp.dot(own_rows.astype(bf16), earlier, preferred_element_type=f32)
    total = jnp.sum(own_rows, axis=1, keepdims=True)
    index = lax.broadcasted_iota(jnp.int32, (8, count), 1)
    spot = jnp.where(own_rows > 0.0, own_before, total + index.astype(f32) - own_before)
    chosen = jnp.where(rows == spot[:1].astype(jnp.int32), 1.0, 0.0).astype(bf16)
    kind = lax.broadcasted_iota(jnp.int32, (8, count), 0)
    values = jnp.where(kind == 0, (index // slots).astype(f32), jnp.broadcast_to(source, (8, count)))
    values = lax.dot_general(
        values.astype(bf16), chosen, (((1,), (1,)), ((), ())), preferred_element_type=f32
    )
    pairs_ref[...] = jnp.where(kind == 2, total, values).astype(jnp.int32)
    pairs_ref[4 : 4 + partners, :leaves] = far_slots


def near_pairs(begin, end, base_slot, pairs_ref, target_ref, source_ref, charge_ref, tail_ref, out_ref, high_ref, low_ref):
    scen = out_ref.shape[1]

    def generate(pair, slot):
        pair = jnp.minimum(pair, end * chunk - 1)
        square = jnp.dot(
            source_ref[pairs_ref[1, pair] - base_slot],
            target_ref[pairs_ref[0, pair]],
            preferred_element_type=f32,
        )
        entry = lax.rsqrt(square)
        high = entry.astype(bf16)
        high_ref[slot] = high
        low_ref[slot] = (entry - high.astype(f32)).astype(fine)

    def apply(pair, slot):
        target = pairs_ref[0, pair]
        source = pairs_ref[1, pair] - base_slot
        first = jnp.dot(charge_ref[source], high_ref[slot], preferred_element_type=f32)
        second = jnp.dot(tail_ref[source], low_ref[slot], preferred_element_type=f32)
        out_ref[target] += (
            first[:scen] + first[scen:] + (second[:scen] + second[scen:]) * (1.0 / (entry_scale * fine_scale))
        )

    @pl.when(begin < end)
    def _():
        for step in range(ahead):
            generate(begin * chunk + step, step)

        def body(step, carry):
            for half in range(2):
                base = step * chunk + half * ahead
                for lane in range(ahead):
                    generate(base + ahead + lane, (1 - half) * ahead + lane)
                    apply(base + lane, half * ahead + lane)
            return carry

        lax.fori_loop(begin, end, body, 0)


def own_chunks(pairs_ref):
    return jnp.minimum(own_steps, pairs_ref[2, 0] // chunk)


def own_kernel(pairs_ref, target_ref, source_ref, charge_ref, tail_ref, out_ref, high_ref, low_ref):
    out_ref[...] = jnp.zeros_like(out_ref)
    near_pairs(
        0, own_chunks(pairs_ref), out_ref.shape[0], pairs_ref, target_ref, source_ref, charge_ref,
        tail_ref, out_ref, high_ref, low_ref,
    )


def rest_kernel(
    cluster_ref, pairs_ref, own_ref, chip_ref, side_ref, coupling_ref, start_ref, out_ref, local_ref,
    target_ref, source_ref, charge_ref, tail_ref, coef_ref, high_ref, low_ref,
):
    leaves, scen, panels = out_ref.shape
    rank = local_ref.shape[2]
    coord_row = leaves * scen
    coef_row = coord_row + leaves * dims

    def coords_of(pack_ref):
        return [
            pack_ref[coord_row + axis * leaves : coord_row + (axis + 1) * leaves]
            for axis in range(dims)
        ]

    own_coords = coords_of(own_ref)
    origin = [jnp.mean(c) for c in own_coords]
    stage_coords(own_coords, origin, False, target_ref, 0)
    odd = cluster_ref[0] & 1
    for pack_ref, place in ((own_ref, 1), (chip_ref, 2 - 2 * odd), (side_ref, 2 * odd)):
        base = place * leaves
        stage_coords(coords_of(pack_ref), origin, True, source_ref, base)
        for leaf in range(leaves):
            stage_charge(pack_ref[leaf * scen : (leaf + 1) * scen], charge_ref, tail_ref, base + leaf)
            coef_ref[base + leaf] = pack_ref[coef_place(leaf, scen, rank, panels, coef_row)]
    for leaf in range(leaves):
        total = jnp.zeros((scen, rank), f32)
        for partner in range(coupling_ref.shape[1]):
            total = total + dot_split(coef_ref[pairs_ref[4 + partner, leaf]], coupling_ref[leaf, partner], 1)
        local_ref[leaf] = total
    out_ref[...] = start_ref[...]
    near_pairs(
        own_chunks(pairs_ref), pairs_ref.shape[1] // chunk, 0, pairs_ref, target_ref, source_ref,
        charge_ref, tail_ref, out_ref, high_ref, low_ref,
    )


def far_kernel(
    cluster_ref, branch_idx_ref, local_ref, nodes_ref, down_ref, row_ref, transfer_ref, down_transfer_ref,
    sibling_ref, branch_ref, near_ref, out_ref,
):
    leaves, scen, panels = near_ref.shape
    rank = down_ref.shape[1]
    levels = transfer_ref.shape[1]
    branches, clusters = nodes_ref.shape[:2]
    cluster_idx, branch_idx = cluster_ref[0], branch_idx_ref[0]
    downward = jnp.zeros((scen, rank), f32)
    for other in range(branches - 1):
        partner = lax.rem(branch_idx + 1 + other, branches)
        root = jnp.sum(nodes_ref[partner], axis=0)[:, rank:]
        downward = downward + dot_split(root, branch_ref[0, other], 1)
    current = nodes_ref[branch_idx][:, :, :rank]
    siblings = []
    for level in range(levels):
        width = clusters >> level
        place = cluster_idx >> level
        siblings.append((current, place ^ 1))
        pairs = current.reshape(width // 2, 2 * scen, rank)
        left = pairs[:, :scen].reshape(width // 2 * scen, rank)
        right = pairs[:, scen:].reshape(width // 2 * scen, rank)
        current = dot_split(left, transfer_ref[0, level, 0], 1) + dot_split(
            right, transfer_ref[0, level, 1], 1
        )
        current = current.reshape(width // 2, scen, rank)
    for level in reversed(range(levels)):
        nodes, place = siblings[level]
        chosen = lax.broadcasted_iota(jnp.int32, (nodes.shape[0], 1, 1), 0) == place
        sibling = jnp.sum(jnp.where(chosen, nodes, 0.0), axis=0)
        parity = (cluster_idx >> level) & 1
        downward = dot_split(sibling, sibling_ref[0, level, parity], 1) + dot_split(
            downward, down_transfer_ref[0, level, parity], 1
        )
    for leaf in range(leaves):
        total = local_ref[leaf] + dot_split(downward, down_ref[leaf], 1)
        out_ref[leaf] = near_ref[leaf] + dot_split(total, row_ref[leaf], 0)


def on_device(
    charges, coords, areas, col_basis, row_basis, leaf_up, leaf_down, leaf_coupling,
    up_transfer, down_transfer, sibling_coupling, branch_coupling, near_list, far_list,
):
    leaves, scen, panels = charges.shape
    rank = col_basis.shape[1]
    clusters, branches = lax.axis_size("cluster"), lax.axis_size("branch")
    cluster_idx = lax.axis_index("cluster").reshape(1).astype(jnp.int32)
    branch_idx = lax.axis_index("branch").reshape(1).astype(jnp.int32)
    count = near_list.size
    pack_rows = leaves * scen + leaves * dims + leaves * scen * rank // panels

    def stages(places):
        return (
            pltpu.VMEM((places * leaves, panels, depth), bf16),
            pltpu.VMEM((places * leaves, 2 * scen, panels), bf16),
            pltpu.VMEM((places * leaves, 2 * scen, panels), wide),
        )

    slots = [pltpu.VMEM((chunk, panels, panels), kind) for kind in (bf16, fine)]
    pack, nodes, pairs, target, *own_stages = pl.pallas_call(
        prep_kernel,
        out_shape=(
            jax.ShapeDtypeStruct((pack_rows, panels), f32),
            jax.ShapeDtypeStruct((branches * clusters * scen, 2 * rank), f32),
            jax.ShapeDtypeStruct((8, count), jnp.int32),
            pltpu.VMEM((leaves, depth, panels), bf16),
            *stages(1),
        ),
        in_specs=[smem] + [vmem] * 8,
        out_specs=(vmem,) * 7,
        compiler_params=large,
        name="prep",
    )(
        cluster_idx, charges, coords.transpose(1, 0, 2), areas, col_basis, leaf_up, up_transfer,
        near_list, far_list.T,
    )

    chip = lax.ppermute(pack, "cluster", [(i, i ^ 1) for i in range(clusters)])
    across = [(i, i + 1) for i in range(1, clusters - 1, 2)]
    side = lax.ppermute(pack, "cluster", across + [(j, i) for i, j in across])
    nodes = lax.all_to_all(nodes, ("branch", "cluster"), 0, 0, tiled=True)
    nodes = nodes.reshape(branches, clusters, scen, 2 * rank)

    kept = pltpu.VMEM((leaves, scen, panels), f32)
    entries = count * panels * panels

    def cost(share):
        return pl.CostEstimate(
            flops=int(entries * 80 * share), bytes_accessed=2**20, transcendentals=int(entries * share)
        )

    near_part = pl.pallas_call(
        own_kernel,
        out_shape=kept,
        in_specs=[smem] + [vmem] * 4,
        out_specs=vmem,
        scratch_shapes=slots,
        compiler_params=params,
        cost_estimate=cost(0.3),
        name="near_own",
    )(pairs, target, *own_stages)
    near_part, local = pl.pallas_call(
        rest_kernel,
        out_shape=(kept, pltpu.VMEM((leaves, scen, rank), f32)),
        in_specs=[smem] * 2 + [vmem] * 5,
        out_specs=(vmem,) * 2,
        scratch_shapes=[
            pltpu.VMEM((leaves, depth, panels), bf16),
            *stages(3),
            pltpu.VMEM((3 * leaves, scen, rank), f32),
            *slots,
        ],
        compiler_params=params,
        cost_estimate=cost(0.7),
        name="near_rest",
    )(cluster_idx, pairs, pack, chip, side, leaf_coupling, near_part)
    return pl.pallas_call(
        far_kernel,
        out_shape=jax.ShapeDtypeStruct((leaves, scen, panels), f32),
        in_specs=[smem] * 2 + [vmem] * 9,
        out_specs=vmem,
        compiler_params=params,
        name="far",
    )(
        cluster_idx, branch_idx, local, nodes, leaf_down, row_basis, up_transfer, down_transfer,
        sibling_coupling, branch_coupling, near_part,
    )


def solution(mesh):
    leaf3 = P(("branch", "cluster"), None, None)
    leaf2 = P(("branch", "cluster"), None)
    leaf4 = P(("branch", "cluster"), None, None, None)
    tree = P("branch", None, None, None, None)
    in_specs = (
        leaf3, leaf3, leaf2, leaf3, leaf3, leaf3, leaf3, leaf4,
        tree, tree, tree, P("branch", None, None, None), leaf2, leaf2,
    )
    return jax.shard_map(
        on_device, mesh=mesh, in_specs=in_specs, out_specs=leaf3, check_vma=False
    )
```

time: 67.4 us -> 45.2 us (0.67)
  the two profiles are of different devices: /device:TPU:5 before, /device:TPU:9 now
where the time goes in v2:
time: 45.2 us; the launch traced here: 45 us
  Pallas kernels  28.7 us (63%)
  starting transfers between devices  9.91 us (22%)
  waiting for transfers between devices  3.78 us (8%)
  local copies, waits for them, and re-layouts  2.49 us (6%)
    pallas_call x1, Pallas kernels, on_device(): pl.pallas_call(rest_kernel, out_shape=(kept, pltpu.VMEM((leaves, scen, ra...  14.1 us
    all_to_all x1, starting transfers between devices, on_device(): nodes = lax.all_to_all(nodes, ('branch', 'cluster'), 0, 0, tiled=True)  6.36 us
    pallas_call x1, Pallas kernels, on_device(): pl.pallas_call(own_kernel, out_shape=kept, in_specs=[smem] + [vmem] * 4,...  6.32 us
    pallas_call x1, Pallas kernels, on_device(): pl.pallas_call(far_kernel, out_shape=jax.ShapeDtypeStruct((leaves, scen,...  4.38 us
    pallas_call x1, Pallas kernels, on_device(): pl.pallas_call(prep_kernel, out_shape=(jax.ShapeDtypeStruct((pack_rows, p...  3.84 us
    ppermute x1, waiting for transfers between devices, on_device(): side = lax.ppermute(pack, 'cluster', across + [(j, i) for i, j in across])  3.77 us
    ppermute x1, starting transfers between devices, on_device(): side = lax.ppermute(pack, 'cluster', across + [(j, i) for i, j in across])  3.34 us
    unnamed x24, local copies, waits for them, and re-layouts  2.49 us
  transfers between devices with their start and end apart: 3, of which 1 were waited for; matrix products, arithmetic and copies ran while one was open for 0% of the time, Pallas kernels for 45%

profile of v2, /device:TPU:9, one launch (start us, length us, event | category | flops | bytes accessed | tf_op | source)
XLA Modules:
  0.0 45.0 jit_solution(15172611035198916718)
XLA Ops:
  0.0 3.8 %prep.1 = (f32[368,256]{1,0:T(8,128)}, f32[512,128]{1,0:T(8,128)}, s32[8,256]{1,0:T(8,128)}, bf16[16,32,256]{2,1,0:T(8,128)(2,1)S(1)}, bf16[16,256,32]{2,1,0:T(8...) custom-call(s32[1]{0:T(128)} %bitcast.cluster_ref, f32[16,16,256]{2,1,0:T(8,128)} %charges_ref.1, ...), custom_call_target="tpu_custom_call" | custom-call | tf_op jit(solution)/shard_map/prep/pallas_call | solution.py:317
  3.8 6.4 %all-to-all-start = ((f32[32,16,128]{2,1,0:T(8,128)}), f32[32,16,128]{2,1,0:T(8,128)S(1)}, u32[]{:S(2)}, u32[]{:S(2)}) async-start(f32[32,16,128]{2,1,0:T(8,128)} %bitcast.7), calls=%async_computation | async-start | bytes 524288 | tf_op jit(solution)/shard_map/all_to_all | solution.py:338
  10.2 3.3 %collective-permute-start.1 = (f32[368,256]{1,0:T(8,128)}, f32[368,256]{1,0:T(8,128)S(1)}, u32[]{:S(2)}, u32[]{:S(2)}) collective-permute-start(f32[368,256]{1,0:T(8,128)} %get-tuple-element.15.own_ref), channel_id=1, source_target_pairs={{1,2},{3,4},{5,6},{7,8},{9,10},{11,12},{13,14},{2,1},{4,3},{6,5},{... | collective-permute-start | bytes 1130504 | tf_op jit(solution)/shard_map/ppermute | solution.py:337
  13.5 0.2 collective-permute-start
  13.8 0.0 copy-start.10
  13.8 0.7 %copy-done.10 = s32[8,256]{1,0:T(8,128)S(1)} copy-done((s32[8,256]{1,0:T(8,128)S(1)}, s32[8,256]{1,0:T(8,128)}, u32[]{:S(2)}) %copy-start.10) | copy-done | bytes 8216
  14.5 0.0 copy-start.6
  14.5 0.0 copy-start.7
  14.5 0.0 copy-start.11
  14.5 6.3 %near_own.1.start_ref = f32[16,16,256]{2,1,0:T(8,128)S(1)} custom-call(s32[8,256]{1,0:T(8,128)S(1)} %copy-done.10, bf16[16,32,256]{2,1,0:T(8,128)(2,1)S(1)} %get-tuple-element.16.target_ref, bf16[16,256,32]{2,1,0:T(8,128)(2,1)S(1)} %get-tuple-element.17.source_ref, bf16[16,32,256]{2,1,0:T(8,128)(2,1)S(1)} %get-tuple-element.18.charge_ref, ...), custom_call_target="tpu_custom_call" | custom-call | flops 402653184 | bytes 1048576 | tf_op jit(solution)/shard_map/near_own/pallas_call | solution.py:349
  20.8 0.0 copy-start
  20.8 0.0 copy-start.1
  20.8 0.0 copy-start.2
  20.8 0.0 copy-start.3
  20.8 0.0 copy-start.4
  20.8 0.0 copy-start.5
  20.9 3.8 %collective-permute-done.1.side_ref = f32[368,256]{1,0:T(8,128)S(1)} collective-permute-done((f32[368,256]{1,0:T(8,128)}, f32[368,256]{1,0:T(8,128)S(1)}, u32[]{:S(2)}, u32[]{:S(2)}) %collective-permute-start.1) | collective-permute-done | bytes 376864 | tf_op jit(solution)/shard_map/ppermute | solution.py:337
  24.6 0.0 collective-permute-done.chip_ref
  24.6 0.8 %copy-done.8 = f32[368,256]{1,0:T(8,128)} copy-done((f32[368,256]{1,0:T(8,128)}, f32[368,256]{1,0:T(8,128)S(1)}, u32[]{:S(2)}) %copy-start.8) | copy-done | bytes 376856
  25.4 0.0 copy-done.6
  25.4 0.0 copy-done.7
  25.4 0.0 copy-done.11
  25.4 1.0 %copy-done.9 = f32[368,256]{1,0:T(8,128)S(1)} copy-done((f32[368,256]{1,0:T(8,128)S(1)}, f32[368,256]{1,0:T(8,128)}, u32[]{:S(2)}) %copy-start.9) | copy-done | bytes 376856
  26.4 14.1 %near_rest.1 = (f32[16,16,256]{2,1,0:T(8,128)S(1)}, f32[16,16,64]{2,1,0:T(8,128)S(1)}) custom-call(s32[1]{0:T(128)} %bitcast.cluster_ref, s32[8,256]{1,0:T(8,128)S(1)} %copy-done.11, f32[368,256]{1,0:T(8,128)S(1)} %copy-done.7, f32[368,256]{1,0:T(8,128)S(1)} %copy-done.9, f32[368,256]{1,0:T(8,128)S(1)} %collective-permute-done.1.side_ref, ...), custom_call_target="tpu_custom_call" | custom-call | flops 939524096 | bytes 1048576 | tf_op jit(solution)/shard_map/near_rest/pallas_call | solution.py:359
  40.5 0.0 all-to-all-done
  40.5 0.0 copy-done
  40.5 0.0 copy-done.1
  40.6 0.0 copy-done.2
  40.6 0.0 copy-done.3
  40.6 0.0 copy-done.4
  40.6 0.0 copy-done.5
  40.6 4.4 %far.1 = f32[16,16,256]{2,1,0:T(8,128)} custom-call(s32[1]{0:T(128)} %bitcast.cluster_ref, s32[1]{0:T(128)} %bitcast.1.branch_idx_ref, f32[16,16,64]{2,1,0:T(8,128)S(1)} %get-tuple-element.20.local_ref, f32[2,16,16,128]{3,2,1,0:T(8,128)S(1)} %bitcast.6, f32[16,64,64]{2,1,0:T(8,128)S(1)} %copy-done.2, f32[16,64,256]{2,1,0:T(8,128)S(1)} %copy-done, ...), custom_call_target="tpu_custom_call" | custom-call | tf_op jit(solution)/shard_map/far/pallas_call | solution.py:374
  (2 shorter events, 0.0 us)
Async XLA Ops:
  3.8 36.7 %all-to-all-start = ((f32[32,16,128]{2,1,0:T(8,128)}), f32[32,16,128]{2,1,0:T(8,128)S(1)}, u32[]{:S(2)}, u32[]{:S(2)}) async-start(f32[32,16,128]{2,1,0:T(8,128)} %bitcast.7), calls=%async_computation | async-start | bytes 524288 | tf_op jit(solution)/shard_map/all_to_all | solution.py:338
  10.2 14.4 %collective-permute-start.1 = (f32[368,256]{1,0:T(8,128)}, f32[368,256]{1,0:T(8,128)S(1)}, u32[]{:S(2)}, u32[]{:S(2)}) collective-permute-start(f32[368,256]{1,0:T(8,128)} %get-tuple-element.15.own_ref), channel_id=1, source_target_pairs={{1,2},{3,4},{5,6},{7,8},{9,10},{11,12},{13,14},{2,1},{4,3},{6,5},{... | collective-permute-start | bytes 1130504 | tf_op jit(solution)/shard_map/ppermute | solution.py:337
  13.5 11.1 %collective-permute-start = (f32[368,256]{1,0:T(8,128)}, f32[368,256]{1,0:T(8,128)S(1)}, u32[]{:S(2)}, u32[]{:S(2)}) collective-permute-start(f32[368,256]{1,0:T(8,128)} %get-tuple-element.15.own_ref), channel_id=1, source_target_pairs={{0,1},{1,0},{2,3},{3,2},{4,5},{5,4},{6,7},{7,6},{8,9},{9,8},{10,11... | collective-permute-start | bytes 1130504 | tf_op jit(solution)/shard_map/ppermute | solution.py:335
  13.8 0.7 %copy-start.10 = (s32[8,256]{1,0:T(8,128)S(1)}, s32[8,256]{1,0:T(8,128)}, u32[]{:S(2)}) copy-start(s32[8,256]{1,0:T(8,128)} %get-tuple-element.14.pairs_ref) | copy-start | bytes 24580
  14.5 10.9 %copy-start.6 = (f32[16,4,64,64]{3,2,1,0:T(8,128)S(1)}, f32[16,4,64,64]{3,2,1,0:T(8,128)}, u32[]{:S(2)}) copy-start(f32[16,4,64,64]{3,2,1,0:T(8,128)} %coupling_ref.1) | copy-start | bytes 3145732
  14.5 10.9 %copy-start.7 = (f32[368,256]{1,0:T(8,128)S(1)}, f32[368,256]{1,0:T(8,128)}, u32[]{:S(2)}) copy-start(f32[368,256]{1,0:T(8,128)} %get-tuple-element.15.own_ref) | copy-start | bytes 1130500
  14.5 10.9 %copy-start.11 = (s32[8,256]{1,0:T(8,128)S(1)}, s32[8,256]{1,0:T(8,128)}, u32[]{:S(2)}) copy-start(s32[8,256]{1,0:T(8,128)} %get-tuple-element.14.pairs_ref) | copy-start | bytes 24580
  20.8 19.8 %copy-start = (f32[16,64,256]{2,1,0:T(8,128)S(1)}, f32[16,64,256]{2,1,0:T(8,128)}, u32[]{:S(2)}) copy-start(f32[16,64,256]{2,1,0:T(8,128)} %row_ref.1) | copy-start | bytes 3145732
  20.8 19.8 %copy-start.1 = (f32[1,4,2,64,64]{4,3,2,1,0:T(8,128)S(1)}, f32[1,4,2,64,64]{4,3,2,1,0:T(8,128)}, u32[]{:S(2)}) copy-start(f32[1,4,2,64,64]{4,3,2,1,0:T(8,128)} %transfer_ref.3) | copy-start | bytes 393220
  20.8 19.7 %copy-start.2 = (f32[16,64,64]{2,1,0:T(8,128)S(1)}, f32[16,64,64]{2,1,0:T(8,128)}, u32[]{:S(2)}) copy-start(f32[16,64,64]{2,1,0:T(8,128)} %down_ref.1) | copy-start | bytes 786436
  20.8 19.7 %copy-start.3 = (f32[1,4,2,64,64]{4,3,2,1,0:T(8,128)S(1)}, f32[1,4,2,64,64]{4,3,2,1,0:T(8,128)}, u32[]{:S(2)}) copy-start(f32[1,4,2,64,64]{4,3,2,1,0:T(8,128)} %down_transfer_ref.1) | copy-start | bytes 393220
  20.8 19.7 %copy-start.4 = (f32[1,4,2,64,64]{4,3,2,1,0:T(8,128)S(1)}, f32[1,4,2,64,64]{4,3,2,1,0:T(8,128)}, u32[]{:S(2)}) copy-start(f32[1,4,2,64,64]{4,3,2,1,0:T(8,128)} %sibling_ref.1) | copy-start | bytes 393220
  20.8 19.7 %copy-start.5 = (f32[1,1,64,64]{3,2,1,0:T(8,128)S(1)}, f32[1,1,64,64]{3,2,1,0:T(8,128)}, u32[]{:S(2)}) copy-start(f32[1,1,64,64]{3,2,1,0:T(8,128)} %branch_ref.1) | copy-start | bytes 49156
  24.6 0.8 %copy-start.8 = (f32[368,256]{1,0:T(8,128)}, f32[368,256]{1,0:T(8,128)S(1)}, u32[]{:S(2)}) copy-start(f32[368,256]{1,0:T(8,128)S(1)} %collective-permute-done.chip_ref) | copy-start | bytes 1130500
  25.4 1.0 %copy-start.9 = (f32[368,256]{1,0:T(8,128)S(1)}, f32[368,256]{1,0:T(8,128)}, u32[]{:S(2)}) copy-start(f32[368,256]{1,0:T(8,128)} %copy-done.8) | copy-start | bytes 1130500

commit v3 on v2

v3 whole, which is shorter than its diff:
```python
import functools
import math

import jax
import jax.numpy as jnp
from jax import lax
from jax.experimental import pallas as pl
from jax.experimental.pallas import tpu as pltpu
from jax.sharding import PartitionSpec as P

f32, bf16 = jnp.float32, jnp.bfloat16
reg_square = 0.01
inv_four_pi = 0.25 / math.pi
dims = 3
ahead = 8
chunk = 2 * ahead
vmem = pl.BlockSpec(memory_space=pltpu.VMEM)
smem = pl.BlockSpec(memory_space=pltpu.SMEM)
anywhere = pl.BlockSpec(memory_space=pl.ANY)
params = pltpu.CompilerParams(vmem_limit_bytes=24 * 2**20)
large = pltpu.CompilerParams(vmem_limit_bytes=58 * 2**20)
lines = 4
depth = 6 * 2 * lines
fine, wide = jnp.float8_e4m3fn, jnp.float8_e5m2
entry_scale, fine_scale = 2.0**13, 2.0**15
own_steps = 5


def split(x):
    high = x.astype(bf16)
    return high, (x - high.astype(f32)).astype(bf16)


def split_three(x):
    high, rest = x.astype(bf16), None
    rest = x - high.astype(f32)
    middle = rest.astype(bf16)
    return high, middle, (rest - middle.astype(f32)).astype(bf16)


def dot_split(a, b, contract):
    rows = a.shape[0]
    a_high, a_low = split(a)
    b_high, b_low = split(b)
    numbers = (((1,), (contract,)), ((), ()))
    first = lax.dot_general(
        jnp.concatenate([a_high, a_low], axis=0), b_high, numbers, preferred_element_type=f32
    )
    second = lax.dot_general(a_high, b_low, numbers, preferred_element_type=f32)
    return first[:rows] + first[rows:] + second


def coord_tiles(pack_ref, first_row, tiles):
    return [pack_ref[first_row + 2 * lines * i : first_row + 2 * lines * (i + 1)] for i in range(tiles)]


def origin_tile(tiles):
    total = sum(jnp.sum(tile, axis=1, keepdims=True) for tile in tiles)
    total = total + pltpu.roll(total, lines, 0)
    return total * (1.0 / (2 * len(tiles) * tiles[0].shape[1]))


def centred(tile, origin):
    line = lax.broadcasted_iota(jnp.int32, tile.shape, 0) & (lines - 1)
    coords = (tile - origin) * (1.0 / entry_scale)
    square = coords * coords
    norm = pltpu.roll(square, 1, 0) + pltpu.roll(square, 2, 0) + pltpu.roll(square, 3, 0)
    return coords, norm, line == dims


def stage_sources(tiles, origin, source_ref, base):
    for i, tile in enumerate(tiles):
        coords, norm, spare = centred(tile, origin)
        high, middle, low = (x.astype(f32) for x in split_three(jnp.where(spare, norm, coords)))
        high_one, middle_one = jnp.where(spare, 1.0, high), jnp.where(spare, 1.0, middle)
        rows = jnp.concatenate([high, middle, high_one, low, high_one, middle_one], axis=0)
        source_ref[base + i] = rows.T.astype(bf16)


def stage_targets(tiles, origin, target_ref):
    for i, tile in enumerate(tiles):
        coords, norm, spare = centred(tile, origin)
        tile = jnp.where(spare, norm + reg_square / entry_scale**2, -2.0 * coords)
        high, middle, low = (x.astype(f32) for x in split_three(tile))
        high_one = jnp.where(spare, 1.0, high)
        rows = [
            high_one, high_one, jnp.where(spare, high, middle), high_one, jnp.where(spare, middle, low),
            jnp.where(spare, low, middle),
        ]
        first = lax.broadcasted_iota(jnp.int32, tile.shape, 0) < lines
        for half in range(2):
            mine = [jnp.where(first if half == 0 else jnp.logical_not(first), row, 0.0) for row in rows]
            other = [pltpu.roll(row, lines, 0) for row in mine]
            for place in range(2):
                chosen = mine if place == half else other
                target_ref[(2 * i + half) * 2 + place] = jnp.concatenate(chosen, axis=0).astype(bf16)


def stage_charge(weighted, charge_ref, tail_ref, slot):
    scen = weighted.shape[0]
    high, low = split(weighted * (1.0 / entry_scale))
    charge_ref[slot, :scen] = high
    charge_ref[slot, scen:] = low
    weighted = weighted * fine_scale
    high = weighted.astype(wide)
    low = (weighted - high.astype(f32)).astype(wide)
    tail_ref[slot] = jnp.concatenate([high.astype(f32), low.astype(f32)], axis=0).astype(wide)


def coef_place(leaf, scen, rank, panels, first_row):
    per_row = panels // rank
    row = first_row + leaf // per_row * scen
    lane = leaf % per_row * rank
    return slice(row, row + scen), slice(lane, lane + rank)


def prep_kernel(
    cluster_ref, branch_ref, charges_ref, coords_ref, areas_ref, col_ref, up_ref, transfer_ref, near_ref, far_ref,
    pack_ref, terms_ref, pairs_ref, target_ref, source_ref, charge_ref, tail_ref,
):
    leaves, scen, panels = charges_ref.shape
    rank = col_ref.shape[1]
    coord_row = leaves * scen
    coef_row = coord_row + leaves * lines

    path = None
    for level in range(transfer_ref.shape[1]):
        matrix = transfer_ref[0, level, (cluster_ref[0] >> level) & 1]
        path = matrix if path is None else dot_split(matrix, path, 0)

    for leaf in range(leaves):
        charge = charges_ref[leaf]
        weighted = charge * (areas_ref[leaf : leaf + 1] * inv_four_pi)
        pack_ref[leaf * scen : (leaf + 1) * scen] = weighted
        stage_charge(weighted, charge_ref, tail_ref, leaf)
        pack_ref[coef_place(leaf, scen, rank, panels, coef_row)] = dot_split(charge, col_ref[leaf], 1)
    node = jnp.zeros((scen, rank), f32)
    per_row = panels // rank
    for group in range(leaves // per_row):
        coefs = pack_ref[coef_row + group * scen : coef_row + (group + 1) * scen]
        ups = jnp.concatenate([up_ref[group * per_row + i] for i in range(per_row)], axis=1)
        node = node + dot_split(coefs, ups, 1)
    half = scen // 2
    node, root = (
        jnp.concatenate([x[:half], x[half:]], axis=1) for x in (node, dot_split(node, path, 1))
    )
    branches = terms_ref.shape[0]
    for branch in range(branches):
        term = jnp.where(branch == branch_ref[0], node, root)
        for cluster in range(terms_ref.shape[1]):
            terms_ref[branch, cluster] = term
    nothing = jnp.zeros((1, panels), f32)
    for leaf in range(leaves):
        rows = [coords_ref[axis, leaf : leaf + 1] for axis in range(dims)] + [nothing]
        pack_ref[coord_row + lines * leaf : coord_row + lines * (leaf + 1)] = jnp.concatenate(rows, axis=0)
    tiles = coord_tiles(pack_ref, coord_row, leaves // 2)
    origin = origin_tile(tiles)
    stage_targets(tiles, origin, target_ref)
    stage_sources(tiles, origin, source_ref, 0)

    slots = near_ref.shape[1]
    count = leaves * slots
    near = near_ref[...]
    base = near[0:1, 0:1] - leaves

    def flat(table):
        n = table.shape[1]
        spread = jnp.where(
            lax.rem(lax.broadcasted_iota(jnp.int32, (n, count), 1), n)
            == lax.broadcasted_iota(jnp.int32, (n, count), 0), 1.0, 0.0
        )
        wide = jnp.dot(table.astype(f32).astype(bf16), spread.astype(bf16), preferred_element_type=f32)
        mine = lax.broadcasted_iota(jnp.int32, (leaves, count), 1) // n == lax.broadcasted_iota(
            jnp.int32, (leaves, count), 0
        )
        return jnp.sum(jnp.where(mine, wide, 0.0), axis=0, keepdims=True)

    source = flat(near - base)
    partners = far_ref.shape[0]
    far_slots = far_ref[...].astype(jnp.int32) - jnp.broadcast_to(base, far_ref.shape)
    own_rows = jnp.broadcast_to(
        jnp.where((source >= leaves) & (source < 2 * leaves), 1.0, 0.0), (8, count)
    )
    rows = lax.broadcasted_iota(jnp.int32, (count, count), 0)
    cols = lax.broadcasted_iota(jnp.int32, (count, count), 1)
    earlier = jnp.where(rows < cols, 1.0, 0.0).astype(bf16)
    own_before = jnp.dot(own_rows.astype(bf16), earlier, preferred_element_type=f32)
    total = jnp.sum(own_rows, axis=1, keepdims=True)
    index = lax.broadcasted_iota(jnp.int32, (8, count), 1)
    spot = jnp.where(own_rows > 0.0, own_before, total + index.astype(f32) - own_before)
    chosen = jnp.where(rows == spot[:1].astype(jnp.int32), 1.0, 0.0).astype(bf16)
    kind = lax.broadcasted_iota(jnp.int32, (8, count), 0)
    values = jnp.where(kind == 0, (index // slots).astype(f32), jnp.broadcast_to(source, (8, count)))
    values = lax.dot_general(
        values.astype(bf16), chosen, (((1,), (1,)), ((), ())), preferred_element_type=f32
    )
    pairs_ref[...] = jnp.where(kind == 2, total, values).astype(jnp.int32)
    pairs_ref[4 : 4 + partners, :leaves] = far_slots


def near_pairs(begin, end, base_slot, pairs_ref, target_ref, source_ref, charge_ref, tail_ref, out_ref, high_ref, low_ref):
    scen = out_ref.shape[1]

    def generate(pair, slot):
        pair = jnp.minimum(pair, end * chunk - 1)
        source = pairs_ref[1, pair] - base_slot
        square = jnp.dot(
            source_ref[source >> 1],
            target_ref[2 * pairs_ref[0, pair] + (source & 1)],
            preferred_element_type=f32,
        )
        entry = lax.rsqrt(square)
        high = entry.astype(bf16)
        high_ref[slot] = high
        low_ref[slot] = (entry - high.astype(f32)).astype(fine)

    def apply(pair, slot):
        target = pairs_ref[0, pair]
        source = pairs_ref[1, pair] - base_slot
        first = jnp.dot(charge_ref[source], high_ref[slot], preferred_element_type=f32)
        second = jnp.dot(tail_ref[source], low_ref[slot], preferred_element_type=f32)
        out_ref[target] += (
            first[:scen] + first[scen:] + (second[:scen] + second[scen:]) * (1.0 / (entry_scale * fine_scale))
        )

    @pl.when(begin < end)
    def _():
        for step in range(ahead):
            generate(begin * chunk + step, step)

        def body(step, carry):
            for half in range(2):
                base = step * chunk + half * ahead
                for lane in range(ahead):
                    generate(base + ahead + lane, (1 - half) * ahead + lane)
                    apply(base + lane, half * ahead + lane)
            return carry

        lax.fori_loop(begin, end, body, 0)


def own_chunks(pairs_ref):
    return jnp.minimum(own_steps, pairs_ref[2, 0] // chunk)


def own_kernel(pairs_ref, target_ref, source_ref, charge_ref, tail_ref, out_ref, high_ref, low_ref):
    out_ref[...] = jnp.zeros_like(out_ref)
    near_pairs(
        0, own_chunks(pairs_ref), out_ref.shape[0], pairs_ref, target_ref, source_ref, charge_ref,
        tail_ref, out_ref, high_ref, low_ref,
    )


def rest_kernel(
    cluster_ref, branch_idx_ref, pairs_ref, own_any, chip_any, side_any, coupling_any, terms_any,
    up_any, down_any, sibling_any, branch_any, leaf_down_any, row_any, start_ref, out_ref,
    own_ref, chip_ref, side_ref, coupling_ref, terms_ref, up_ref, down_ref, sibling_ref, branch_ref,
    leaf_down_ref, row_ref, target_ref, source_ref, charge_ref, tail_ref, coef_ref, high_ref, low_ref, sems,
):
    leaves, scen, panels = out_ref.shape
    rank = leaf_down_ref.shape[1]
    branches, clusters = terms_ref.shape[:2]
    levels = up_ref.shape[1]
    coord_row = leaves * scen
    coef_row = coord_row + leaves * lines
    cluster_idx, branch_idx = cluster_ref[0], branch_idx_ref[0]
    refs = (
        own_any, chip_any, side_any, terms_any, up_any, down_any, sibling_any, branch_any, coupling_any,
        leaf_down_any, row_any,
    )
    held = (
        own_ref, chip_ref, side_ref, terms_ref, up_ref, down_ref, sibling_ref, branch_ref, coupling_ref,
        leaf_down_ref, row_ref,
    )
    copies = [pltpu.make_async_copy(ref, to, sems.at[i]) for i, (ref, to) in enumerate(zip(refs, held))]
    for copy in copies:
        copy.start()

    copies[0].wait()
    tiles = coord_tiles(own_ref, coord_row, leaves // 2)
    origin = origin_tile(tiles)
    stage_targets(tiles, origin, target_ref)
    odd = cluster_idx & 1
    for i, (pack_ref, place) in enumerate(((own_ref, 1), (chip_ref, 2 - 2 * odd), (side_ref, 2 * odd))):
        if i:
            copies[i].wait()
        stage_sources(coord_tiles(pack_ref, coord_row, leaves // 2), origin, source_ref, place * (leaves // 2))
        base = place * leaves
        for leaf in range(leaves):
            stage_charge(pack_ref[leaf * scen : (leaf + 1) * scen], charge_ref, tail_ref, base + leaf)
            coef_ref[base + leaf] = pack_ref[coef_place(leaf, scen, rank, panels, coef_row)]
    for copy in copies[3:]:
        copy.wait()

    def unfold(x):
        return jnp.concatenate([x[..., :rank], x[..., rank:]], axis=-2)

    current = unfold(terms_ref[branch_idx])
    sums, chains, chain = [], [], None
    for level in range(levels):
        width = clusters >> level
        chosen = lax.broadcasted_iota(jnp.int32, (width, 1, 1), 0) == (cluster_idx >> level) ^ 1
        sums.append(jnp.sum(jnp.where(chosen, current, 0.0), axis=0))
        if level + 1 < levels:
            couples = current.reshape(width // 2, 2 * scen, rank)
            sides = [
                couples[:, side * scen : (side + 1) * scen].reshape(width // 2 * scen, rank)
                for side in range(2)
            ]
            current = dot_split(sides[0], up_ref[0, level, 0], 1) + dot_split(
                sides[1], up_ref[0, level, 1], 1
            )
            current = current.reshape(width // 2, scen, rank)
        parity = (cluster_idx >> level) & 1
        matrix = sibling_ref[0, level, parity]
        chains.append(matrix if chain is None else dot_split(chain, matrix, 0))
        matrix = down_ref[0, level, parity]
        chain = matrix if chain is None else dot_split(chain, matrix, 0)
    for other in range(branches - 1):
        partner = lax.rem(branch_idx + 1 + other, branches)
        sums.append(unfold(jnp.sum(terms_ref[partner], axis=0)))
        chains.append(dot_split(chain, branch_ref[0, other], 0))
    downward = jnp.zeros((scen, rank), f32)
    for term, matrix in zip(sums, chains):
        downward = downward + dot_split(term, matrix, 1)

    for leaf in range(leaves):
        partners = range(coupling_ref.shape[1])
        coefs = jnp.concatenate([coef_ref[pairs_ref[4 + partner, leaf]] for partner in partners], axis=1)
        matrices = jnp.concatenate([coupling_ref[leaf, partner] for partner in partners], axis=1)
        total = dot_split(coefs, matrices, 1) + dot_split(downward, leaf_down_ref[leaf], 1)
        out_ref[leaf] = start_ref[leaf] + dot_split(total, row_ref[leaf], 0)
    near_pairs(
        own_chunks(pairs_ref), pairs_ref.shape[1] // chunk, 0, pairs_ref, target_ref, source_ref,
        charge_ref, tail_ref, out_ref, high_ref, low_ref,
    )


def on_device(
    charges, coords, areas, col_basis, row_basis, leaf_up, leaf_down, leaf_coupling,
    up_transfer, down_transfer, sibling_coupling, branch_coupling, near_list, far_list,
):
    leaves, scen, panels = charges.shape
    rank = col_basis.shape[1]
    clusters, branches = lax.axis_size("cluster"), lax.axis_size("branch")
    cluster_idx = lax.axis_index("cluster").reshape(1).astype(jnp.int32)
    branch_idx = lax.axis_index("branch").reshape(1).astype(jnp.int32)
    count = near_list.size
    pack_rows = leaves * scen + leaves * lines + leaves * scen * rank // panels

    def stages(places):
        return (
            pltpu.VMEM((places * leaves // 2, panels, depth), bf16),
            pltpu.VMEM((places * leaves, 2 * scen, panels), bf16),
            pltpu.VMEM((places * leaves, 2 * scen, panels), wide),
        )

    slots = [pltpu.VMEM((chunk, panels, panels), kind) for kind in (bf16, fine)]
    terms_shape = (branches, clusters, scen // 2, 2 * rank)
    pack, terms, pairs, target, *own_stages = pl.pallas_call(
        prep_kernel,
        out_shape=(
            jax.ShapeDtypeStruct((pack_rows, panels), f32),
            jax.ShapeDtypeStruct(terms_shape, f32),
            jax.ShapeDtypeStruct((8, count), jnp.int32),
            pltpu.VMEM((2 * leaves, depth, panels), bf16),
            *stages(1),
        ),
        in_specs=[smem] * 2 + [vmem] * 8,
        out_specs=(vmem,) * 7,
        compiler_params=large,
        name="prep",
    )(
        cluster_idx, branch_idx, charges, coords.transpose(1, 0, 2), areas, col_basis, leaf_up, up_transfer,
        near_list, far_list.T,
    )

    chip = lax.ppermute(pack, "cluster", [(i, i ^ 1) for i in range(clusters)])
    across = [(i, i + 1) for i in range(1, clusters - 1, 2)]
    side = lax.ppermute(pack, "cluster", across + [(j, i) for i, j in across])
    terms = terms.reshape(branches * clusters, scen // 2, 2 * rank)
    terms = lax.all_to_all(terms, ("branch", "cluster"), 0, 0, tiled=True)
    terms = terms.reshape(terms_shape)

    kept = pltpu.VMEM((leaves, scen, panels), f32)
    entries = count * panels * panels

    def cost(share):
        return pl.CostEstimate(
            flops=int(entries * 80 * share), bytes_accessed=2**20, transcendentals=int(entries * share)
        )

    stay = functools.partial(pltpu.with_memory_space_constraint, memory_space=pltpu.HBM)
    pairs = stay(pairs)
    near_part = pl.pallas_call(
        own_kernel,
        out_shape=kept,
        in_specs=[smem] + [vmem] * 4,
        out_specs=vmem,
        scratch_shapes=slots,
        compiler_params=params,
        cost_estimate=cost(10),
        name="near_own",
    )(pairs, target, *own_stages)
    operands = (
        stay(pack), chip, side, stay(leaf_coupling), terms, stay(up_transfer), stay(down_transfer),
        stay(sibling_coupling), stay(branch_coupling), stay(leaf_down), stay(row_basis),
    )
    return pl.pallas_call(
        rest_kernel,
        out_shape=jax.ShapeDtypeStruct((leaves, scen, panels), f32),
        in_specs=[smem] * 3 + [anywhere] * len(operands) + [vmem],
        out_specs=vmem,
        scratch_shapes=[
            *(pltpu.VMEM(operand.shape, f32) for operand in operands),
            pltpu.VMEM((2 * leaves, depth, panels), bf16),
            *stages(3),
            pltpu.VMEM((3 * leaves, scen, rank), f32),
            *slots,
            pltpu.SemaphoreType.DMA((len(operands),)),
        ],
        compiler_params=params,
        cost_estimate=cost(10),
        name="near_rest",
    )(cluster_idx, branch_idx, pairs, *operands, near_part)


def solution(mesh):
    leaf3 = P(("branch", "cluster"), None, None)
    leaf2 = P(("branch", "cluster"), None)
    leaf4 = P(("branch", "cluster"), None, None, None)
    tree = P("branch", None, None, None, None)
    in_specs = (
        leaf3, leaf3, leaf2, leaf3, leaf3, leaf3, leaf3, leaf4,
        tree, tree, tree, P("branch", None, None, None), leaf2, leaf2,
    )
    return jax.shard_map(
        on_device, mesh=mesh, in_specs=in_specs, out_specs=leaf3, check_vma=False
    )
```

time: 45.2 us -> 42 us (0.929)
  the two profiles are of different devices: /device:TPU:9 before, /device:TPU:0 now
where the time goes in v3:
time: 42 us; the launch traced here: 41.7 us
  Pallas kernels  30 us (71%)
  starting transfers between devices  9.94 us (24%)
  waiting for transfers between devices  1.76 us (4%)
    pallas_call x1, Pallas kernels, on_device(): pl.pallas_call(rest_kernel, out_shape=jax.ShapeDtypeStruct((leaves, scen,...  19.9 us
    pallas_call x1, Pallas kernels, on_device(): pl.pallas_call(own_kernel, out_shape=kept, in_specs=[smem] + [vmem] * 4,...  6.47 us
    all_to_all x1, starting transfers between devices, on_device(): terms = lax.all_to_all(terms, ('branch', 'cluster'), 0, 0, tiled=True)  4.89 us
    ppermute x1, starting transfers between devices, on_device(): chip = lax.ppermute(pack, 'cluster', [(i, i ^ 1) for i in range(clusters)])  4.37 us
    pallas_call x1, Pallas kernels, on_device(): pl.pallas_call(prep_kernel, out_shape=(jax.ShapeDtypeStruct((pack_rows, p...  3.56 us
    all_to_all x1, waiting for transfers between devices, on_device(): terms = lax.all_to_all(terms, ('branch', 'cluster'), 0, 0, tiled=True)  1.75 us
  transfers between devices with their start and end apart: 3, of which 1 were waited for; matrix products, arithmetic and copies ran while one was open for 0% of the time, Pallas kernels for 16%

profile of v3, /device:TPU:0, one launch (start us, length us, event | category | flops | bytes accessed | tf_op | source)
XLA Modules:
  0.0 41.7 jit_solution(8077291193698451578)
XLA Ops:
  0.0 3.6 %prep.1 = (f32[384,256]{1,0:T(8,128)}, f32[2,16,8,128]{3,2,1,0:T(8,128)}, s32[8,256]{1,0:T(8,128)}, bf16[32,48,256]{2,1,0:T(8,128)(2,1)S(1)}, bf16[8,256,48]{2,1...) custom-call(s32[1]{0:T(128)} %bitcast.cluster_ref, ...), custom_call_target="tpu_custom_call" | custom-call | tf_op jit(solution)/shard_map/prep/pallas_call | solution.py:360
  3.6 0.7 %collective-permute-start.1 = (f32[384,256]{1,0:T(8,128)}, f32[384,256]{1,0:T(8,128)S(1)}, u32[]{:S(2)}, u32[]{:S(2)}) collective-permute-start(f32[384,256]{1,0:T(8,128)} %get-tuple-element.13.own_any), channel_id=1, source_target_pairs={{1,2},{3,4},{5,6},{7,8},{9,10},{11,12},{13,14},{2,1},{4,3},{6,5},{... | collective-permute-start | bytes 1179656 | tf_op jit(solution)/shard_map/ppermute | solution.py:380
  4.2 4.4 %collective-permute-start = (f32[384,256]{1,0:T(8,128)}, f32[384,256]{1,0:T(8,128)S(1)}, u32[]{:S(2)}, u32[]{:S(2)}) collective-permute-start(f32[384,256]{1,0:T(8,128)} %get-tuple-element.13.own_any), channel_id=1, source_target_pairs={{0,1},{1,0},{2,3},{3,2},{4,5},{5,4},{6,7},{7,6},{8,9},{9,8},{10,11... | collective-permute-start | bytes 1179656 | tf_op jit(solution)/shard_map/ppermute | solution.py:378
  8.6 4.9 %all-to-all-start = ((f32[32,8,128]{2,1,0:T(8,128)}), f32[32,8,128]{2,1,0:T(8,128)S(1)}, u32[]{:S(2)}, u32[]{:S(2)}) async-start(f32[32,8,128]{2,1,0:T(8,128)} %bitcast.7), calls=%async_computation | async-start | bytes 262144 | tf_op jit(solution)/shard_map/all_to_all | solution.py:382
  13.5 6.5 %near_own.1.start_ref = f32[16,16,256]{2,1,0:T(8,128)S(1)} custom-call(s32[8,256]{1,0:T(8,128)} %get-tuple-element.12.pairs_ref, bf16[32,48,256]{2,1,0:T(8,128)(2,1)S(1)} %get-tuple-element.15.target_ref, bf16[8,256,48]{2,1,0:T(8,128)(2,1)S(1)} %get-tuple-element.16.source_ref, bf16[16,32,256]{2,1,0:T(8,128)(2,1)S(1)} %get-tuple-element.17.charge_ref, ...), custom_call_target="tpu_custom_call" | custom-call | flops 13421772800 | bytes 1048576 | tf_op jit(solution)/shard_map/near_own/pallas_call | solution.py:395
  20.0 1.8 %all-to-all-done = f32[32,8,128]{2,1,0:T(8,128)S(1)} async-done(((f32[32,8,128]{2,1,0:T(8,128)}), f32[32,8,128]{2,1,0:T(8,128)S(1)}, u32[]{:S(2)}, u32[]{:S(2)}) %all-to-all-start) | async-done | bytes 131104 | tf_op jit(solution)/shard_map/all_to_all | solution.py:382
  21.7 0.0 collective-permute-done.1.side_any
  21.7 0.0 collective-permute-done.chip_any
  21.7 19.9 %near_rest.1 = f32[16,16,256]{2,1,0:T(8,128)} custom-call(s32[1]{0:T(128)} %bitcast.cluster_ref, s32[1]{0:T(128)} %bitcast.1.branch_ref.branch_idx_ref, s32[8,256]{1,0:T(8,128)} %get-tuple-element.12.pairs_ref, f32[384,256]{1,0:T(8,128)} %get-tuple-element.13.own_any, f32[384,256]{1,0:T(8,128)S(1)} %collective-permute-done.chip_any, ...), custom_call_target="tpu_custom_call" | custom-call | flops 13421772800 | bytes 1048576 | tf_op jit(solution)/shard_map/near_rest/pallas_call | solution.py:409
Async XLA Ops:
  3.6 18.2 %collective-permute-start.1 = (f32[384,256]{1,0:T(8,128)}, f32[384,256]{1,0:T(8,128)S(1)}, u32[]{:S(2)}, u32[]{:S(2)}) collective-permute-start(f32[384,256]{1,0:T(8,128)} %get-tuple-element.13.own_any), channel_id=1, source_target_pairs={{1,2},{3,4},{5,6},{7,8},{9,10},{11,12},{13,14},{2,1},{4,3},{6,5},{... | collective-permute-start | bytes 1179656 | tf_op jit(solution)/shard_map/ppermute | solution.py:380
  4.2 17.5 %collective-permute-start = (f32[384,256]{1,0:T(8,128)}, f32[384,256]{1,0:T(8,128)S(1)}, u32[]{:S(2)}, u32[]{:S(2)}) collective-permute-start(f32[384,256]{1,0:T(8,128)} %get-tuple-element.13.own_any), channel_id=1, source_target_pairs={{0,1},{1,0},{2,3},{3,2},{4,5},{5,4},{6,7},{7,6},{8,9},{9,8},{10,11... | collective-permute-start | bytes 1179656 | tf_op jit(solution)/shard_map/ppermute | solution.py:378
  8.6 13.1 %all-to-all-start = ((f32[32,8,128]{2,1,0:T(8,128)}), f32[32,8,128]{2,1,0:T(8,128)S(1)}, u32[]{:S(2)}, u32[]{:S(2)}) async-start(f32[32,8,128]{2,1,0:T(8,128)} %bitcast.7), calls=%async_computation | async-start | bytes 262144 | tf_op jit(solution)/shard_map/all_to_all | solution.py:382

commit v4 on v3

--- a/solution.py
+++ b/solution.py
@@ -198,11 +198,10 @@
     pairs_ref[4 : 4 + partners, :leaves] = far_slots
 
 
-def near_pairs(begin, end, base_slot, pairs_ref, target_ref, source_ref, charge_ref, tail_ref, out_ref, high_ref, low_ref):
+def near_pairs(some, begin, end, base_slot, pairs_ref, target_ref, source_ref, charge_ref, tail_ref, out_ref, high_ref, low_ref):
     scen = out_ref.shape[1]
 
     def generate(pair, slot):
-        pair = jnp.minimum(pair, end * chunk - 1)
         source = pairs_ref[1, pair] - base_slot
         square = jnp.dot(
             source_ref[source >> 1],
@@ -223,8 +222,7 @@
             first[:scen] + first[scen:] + (second[:scen] + second[scen:]) * (1.0 / (entry_scale * fine_scale))
         )
 
-    @pl.when(begin < end)
-    def _():
+    def run():
         for step in range(ahead):
             generate(begin * chunk + step, step)
 
@@ -236,7 +234,18 @@
                     apply(base + lane, half * ahead + lane)
             return carry
 
-        lax.fori_loop(begin, end, body, 0)
+        lax.fori_loop(begin, end - 1, body, 0)
+        base = (end - 1) * chunk
+        for lane in range(ahead):
+            generate(base + ahead + lane, ahead + lane)
+            apply(base + lane, lane)
+        for lane in range(ahead):
+            apply(base + ahead + lane, ahead + lane)
+
+    if some:
+        run()
+    else:
+        pl.when(begin < end)(run)
 
 
 def own_chunks(pairs_ref):
@@ -246,7 +255,7 @@
 def own_kernel(pairs_ref, target_ref, source_ref, charge_ref, tail_ref, out_ref, high_ref, low_ref):
     out_ref[...] = jnp.zeros_like(out_ref)
     near_pairs(
-        0, own_chunks(pairs_ref), out_ref.shape[0], pairs_ref, target_ref, source_ref, charge_ref,
+        out_ref.shape[0] >= chunk, 0, own_chunks(pairs_ref), out_ref.shape[0], pairs_ref, target_ref, source_ref, charge_ref,
         tail_ref, out_ref, high_ref, low_ref,
     )
 
@@ -275,7 +284,6 @@
     copies = [pltpu.make_async_copy(ref, to, sems.at[i]) for i, (ref, to) in enumerate(zip(refs, held))]
     for copy in copies:
         copy.start()
-
     copies[0].wait()
     tiles = coord_tiles(own_ref, coord_row, leaves // 2)
     origin = origin_tile(tiles)
@@ -289,6 +297,11 @@
         for leaf in range(leaves):
             stage_charge(pack_ref[leaf * scen : (leaf + 1) * scen], charge_ref, tail_ref, base + leaf)
             coef_ref[base + leaf] = pack_ref[coef_place(leaf, scen, rank, panels, coef_row)]
+    out_ref[...] = start_ref[...]
+    near_pairs(
+        False, own_chunks(pairs_ref), pairs_ref.shape[1] // chunk, 0, pairs_ref, target_ref, source_ref,
+        charge_ref, tail_ref, out_ref, high_ref, low_ref,
+    )
     for copy in copies[3:]:
         copy.wait()
 
@@ -329,11 +342,7 @@
         coefs = jnp.concatenate([coef_ref[pairs_ref[4 + partner, leaf]] for partner in partners], axis=1)
         matrices = jnp.concatenate([coupling_ref[leaf, partner] for partner in partners], axis=1)
         total = dot_split(coefs, matrices, 1) + dot_split(downward, leaf_down_ref[leaf], 1)
-        out_ref[leaf] = start_ref[leaf] + dot_split(total, row_ref[leaf], 0)
-    near_pairs(
-        own_chunks(pairs_ref), pairs_ref.shape[1] // chunk, 0, pairs_ref, target_ref, source_ref,
-        charge_ref, tail_ref, out_ref, high_ref, low_ref,
-    )
+        out_ref[leaf] += dot_split(total, row_ref[leaf], 0)
 
 
 def on_device(

time: 42 us -> 41.6 us (level)
  Pallas kernels: 30 us -> 29.4 us
    pallas_call x1, Pallas kernels: 19.9 us -> 19.5 us  [on_device(): pl.pallas_call(rest_kernel, out_shape=jax.ShapeDtypeStruct((leaves, scen,...]
  transfers between devices with their start and end apart: 3 -> 3, of which waited for: 1 -> 1; matrix products, arithmetic and copies ran while one was open for 0% -> 0% of each run, Pallas kernels for 16% -> 15%
where the time goes in v4:
time: 41.6 us; the launch traced here: 41.2 us
  Pallas kernels  29.4 us (71%)
  starting transfers between devices  9.94 us (24%)
  waiting for transfers between devices  1.89 us (5%)
    pallas_call x1, Pallas kernels, on_device(): pl.pallas_call(rest_kernel, out_shape=jax.ShapeDtypeStruct((leaves, scen,...  19.5 us
    pallas_call x1, Pallas kernels, on_device(): pl.pallas_call(own_kernel, out_shape=kept, in_specs=[smem] + [vmem] * 4,...  6.33 us
    all_to_all x1, starting transfers between devices, on_device(): terms = lax.all_to_all(terms, ('branch', 'cluster'), 0, 0, tiled=True)  4.89 us
    ppermute x1, starting transfers between devices, on_device(): chip = lax.ppermute(pack, 'cluster', [(i, i ^ 1) for i in range(clusters)])  4.37 us
    pallas_call x1, Pallas kernels, on_device(): pl.pallas_call(prep_kernel, out_shape=(jax.ShapeDtypeStruct((pack_rows, p...  3.56 us
    all_to_all x1, waiting for transfers between devices, on_device(): terms = lax.all_to_all(terms, ('branch', 'cluster'), 0, 0, tiled=True)  1.89 us
  transfers between devices with their start and end apart: 3, of which 1 were waited for; matrix products, arithmetic and copies ran while one was open for 0% of the time, Pallas kernels for 15%

profile of v4, /device:TPU:0, one launch (start us, length us, event | category | flops | bytes accessed | tf_op | source)
XLA Modules:
  0.0 41.2 jit_solution(3731352061987299475)
XLA Ops:
  0.0 3.6 %prep.1 = (f32[384,256]{1,0:T(8,128)}, f32[2,16,8,128]{3,2,1,0:T(8,128)}, s32[8,256]{1,0:T(8,128)}, bf16[32,48,256]{2,1,0:T(8,128)(2,1)S(1)}, bf16[8,256,48]{2,1...) custom-call(s32[1]{0:T(128)} %bitcast.cluster_ref, ...), custom_call_target="tpu_custom_call" | custom-call | tf_op jit(solution)/shard_map/prep/pallas_call | solution.py:369
  3.6 0.7 %collective-permute-start.1 = (f32[384,256]{1,0:T(8,128)}, f32[384,256]{1,0:T(8,128)S(1)}, u32[]{:S(2)}, u32[]{:S(2)}) collective-permute-start(f32[384,256]{1,0:T(8,128)} %get-tuple-element.13.own_any), channel_id=1, source_target_pairs={{1,2},{3,4},{5,6},{7,8},{9,10},{11,12},{13,14},{2,1},{4,3},{6,5},{... | collective-permute-start | bytes 1179656 | tf_op jit(solution)/shard_map/ppermute | solution.py:389
  4.2 4.4 %collective-permute-start = (f32[384,256]{1,0:T(8,128)}, f32[384,256]{1,0:T(8,128)S(1)}, u32[]{:S(2)}, u32[]{:S(2)}) collective-permute-start(f32[384,256]{1,0:T(8,128)} %get-tuple-element.13.own_any), channel_id=1, source_target_pairs={{0,1},{1,0},{2,3},{3,2},{4,5},{5,4},{6,7},{7,6},{8,9},{9,8},{10,11... | collective-permute-start | bytes 1179656 | tf_op jit(solution)/shard_map/ppermute | solution.py:387
  8.6 4.9 %all-to-all-start = ((f32[32,8,128]{2,1,0:T(8,128)}), f32[32,8,128]{2,1,0:T(8,128)S(1)}, u32[]{:S(2)}, u32[]{:S(2)}) async-start(f32[32,8,128]{2,1,0:T(8,128)} %bitcast.7), calls=%async_computation | async-start | bytes 262144 | tf_op jit(solution)/shard_map/all_to_all | solution.py:391
  13.5 6.3 %near_own.1.start_ref = f32[16,16,256]{2,1,0:T(8,128)S(1)} custom-call(s32[8,256]{1,0:T(8,128)} %get-tuple-element.12.pairs_ref, bf16[32,48,256]{2,1,0:T(8,128)(2,1)S(1)} %get-tuple-element.15.target_ref, bf16[8,256,48]{2,1,0:T(8,128)(2,1)S(1)} %get-tuple-element.16.source_ref, bf16[16,32,256]{2,1,0:T(8,128)(2,1)S(1)} %get-tuple-element.17.charge_ref, ...), custom_call_target="tpu_custom_call" | custom-call | flops 13421772800 | bytes 1048576 | tf_op jit(solution)/shard_map/near_own/pallas_call | solution.py:404
  19.9 1.9 %all-to-all-done = f32[32,8,128]{2,1,0:T(8,128)S(1)} async-done(((f32[32,8,128]{2,1,0:T(8,128)}), f32[32,8,128]{2,1,0:T(8,128)S(1)}, u32[]{:S(2)}, u32[]{:S(2)}) %all-to-all-start) | async-done | bytes 131104 | tf_op jit(solution)/shard_map/all_to_all | solution.py:391
  21.7 0.0 collective-permute-done.1.side_any
  21.7 0.0 collective-permute-done.chip_any
  21.7 19.5 %near_rest.1 = f32[16,16,256]{2,1,0:T(8,128)} custom-call(s32[1]{0:T(128)} %bitcast.cluster_ref, s32[1]{0:T(128)} %bitcast.1.branch_ref.branch_idx_ref, s32[8,256]{1,0:T(8,128)} %get-tuple-element.12.pairs_ref, f32[384,256]{1,0:T(8,128)} %get-tuple-element.13.own_any, f32[384,256]{1,0:T(8,128)S(1)} %collective-permute-done.chip_any, ...), custom_call_target="tpu_custom_call" | custom-call | flops 13421772800 | bytes 1048576 | tf_op jit(solution)/shard_map/near_rest/pallas_call | solution.py:418
Async XLA Ops:
  3.6 18.2 %collective-permute-start.1 = (f32[384,256]{1,0:T(8,128)}, f32[384,256]{1,0:T(8,128)S(1)}, u32[]{:S(2)}, u32[]{:S(2)}) collective-permute-start(f32[384,256]{1,0:T(8,128)} %get-tuple-element.13.own_any), channel_id=1, source_target_pairs={{1,2},{3,4},{5,6},{7,8},{9,10},{11,12},{13,14},{2,1},{4,3},{6,5},{... | collective-permute-start | bytes 1179656 | tf_op jit(solution)/shard_map/ppermute | solution.py:389
  4.2 17.5 %collective-permute-start = (f32[384,256]{1,0:T(8,128)}, f32[384,256]{1,0:T(8,128)S(1)}, u32[]{:S(2)}, u32[]{:S(2)}) collective-permute-start(f32[384,256]{1,0:T(8,128)} %get-tuple-element.13.own_any), channel_id=1, source_target_pairs={{0,1},{1,0},{2,3},{3,2},{4,5},{5,4},{6,7},{7,6},{8,9},{9,8},{10,11... | collective-permute-start | bytes 1179656 | tf_op jit(solution)/shard_map/ppermute | solution.py:387
  8.6 13.1 %all-to-all-start = ((f32[32,8,128]{2,1,0:T(8,128)}), f32[32,8,128]{2,1,0:T(8,128)S(1)}, u32[]{:S(2)}, u32[]{:S(2)}) async-start(f32[32,8,128]{2,1,0:T(8,128)} %bitcast.7), calls=%async_computation | async-start | bytes 262144 | tf_op jit(solution)/shard_map/all_to_all | solution.py:391

commit v5 on v4

--- a/solution.py
+++ b/solution.py
@@ -23,7 +23,7 @@
 depth = 6 * 2 * lines
 fine, wide = jnp.float8_e4m3fn, jnp.float8_e5m2
 entry_scale, fine_scale = 2.0**13, 2.0**15
-own_steps = 5
+chip_steps = 8
 
 
 def split(x):
@@ -116,7 +116,7 @@
 
 def prep_kernel(
     cluster_ref, branch_ref, charges_ref, coords_ref, areas_ref, col_ref, up_ref, transfer_ref, near_ref, far_ref,
-    pack_ref, terms_ref, pairs_ref, target_ref, source_ref, charge_ref, tail_ref,
+    pack_ref, terms_ref, pairs_ref,
 ):
     leaves, scen, panels = charges_ref.shape
     rank = col_ref.shape[1]
@@ -132,7 +132,6 @@
         charge = charges_ref[leaf]
         weighted = charge * (areas_ref[leaf : leaf + 1] * inv_four_pi)
         pack_ref[leaf * scen : (leaf + 1) * scen] = weighted
-        stage_charge(weighted, charge_ref, tail_ref, leaf)
         pack_ref[coef_place(leaf, scen, rank, panels, coef_row)] = dot_split(charge, col_ref[leaf], 1)
     node = jnp.zeros((scen, rank), f32)
     per_row = panels // rank
@@ -153,11 +152,6 @@
     for leaf in range(leaves):
         rows = [coords_ref[axis, leaf : leaf + 1] for axis in range(dims)] + [nothing]
         pack_ref[coord_row + lines * leaf : coord_row + lines * (leaf + 1)] = jnp.concatenate(rows, axis=0)
-    tiles = coord_tiles(pack_ref, coord_row, leaves // 2)
-    origin = origin_tile(tiles)
-    stage_targets(tiles, origin, target_ref)
-    stage_sources(tiles, origin, source_ref, 0)
-
     slots = near_ref.shape[1]
     count = leaves * slots
     near = near_ref[...]
@@ -178,16 +172,17 @@
     source = flat(near - base)
     partners = far_ref.shape[0]
     far_slots = far_ref[...].astype(jnp.int32) - jnp.broadcast_to(base, far_ref.shape)
-    own_rows = jnp.broadcast_to(
-        jnp.where((source >= leaves) & (source < 2 * leaves), 1.0, 0.0), (8, count)
+    first = (leaves * (1 - (cluster_ref[0] & 1))).astype(f32)
+    chip_rows = jnp.broadcast_to(
+        jnp.where((source >= first) & (source < first + 2 * leaves), 1.0, 0.0), (8, count)
     )
     rows = lax.broadcasted_iota(jnp.int32, (count, count), 0)
     cols = lax.broadcasted_iota(jnp.int32, (count, count), 1)
     earlier = jnp.where(rows < cols, 1.0, 0.0).astype(bf16)
-    own_before = jnp.dot(own_rows.astype(bf16), earlier, preferred_element_type=f32)
-    total = jnp.sum(own_rows, axis=1, keepdims=True)
+    chip_before = jnp.dot(chip_rows.astype(bf16), earlier, preferred_element_type=f32)
+    total = jnp.sum(chip_rows, axis=1, keepdims=True)
     index = lax.broadcasted_iota(jnp.int32, (8, count), 1)
-    spot = jnp.where(own_rows > 0.0, own_before, total + index.astype(f32) - own_before)
+    spot = jnp.where(chip_rows > 0.0, chip_before, total + index.astype(f32) - chip_before)
     chosen = jnp.where(rows == spot[:1].astype(jnp.int32), 1.0, 0.0).astype(bf16)
     kind = lax.broadcasted_iota(jnp.int32, (8, count), 0)
     values = jnp.where(kind == 0, (index // slots).astype(f32), jnp.broadcast_to(source, (8, count)))
@@ -248,14 +243,37 @@
         pl.when(begin < end)(run)
 
 
-def own_chunks(pairs_ref):
-    return jnp.minimum(own_steps, pairs_ref[2, 0] // chunk)
-
-
-def own_kernel(pairs_ref, target_ref, source_ref, charge_ref, tail_ref, out_ref, high_ref, low_ref):
+def chip_chunks(pairs_ref):
+    return jnp.minimum(chip_steps, pairs_ref[2, 0] // chunk)
+
+
+def chip_kernel(
+    cluster_ref, pairs_ref, own_any, chip_any, out_ref, own_ref, chip_ref, target_ref, source_ref, charge_ref,
+    tail_ref, high_ref, low_ref, sems,
+):
+    leaves, scen, panels = out_ref.shape
+    coord_row = leaves * scen
+    copies = [
+        pltpu.make_async_copy(ref, to, sems.at[i])
+        for i, (ref, to) in enumerate(((own_any, own_ref), (chip_any, chip_ref)))
+    ]
+    for copy in copies:
+        copy.start()
     out_ref[...] = jnp.zeros_like(out_ref)
+    copies[0].wait()
+    tiles = coord_tiles(own_ref, coord_row, leaves // 2)
+    origin = origin_tile(tiles)
+    stage_targets(tiles, origin, target_ref)
+    odd = cluster_ref[0] & 1
+    for i, (pack_ref, place) in enumerate(((own_ref, 1), (chip_ref, 2 - 2 * odd))):
+        if i:
+            copies[i].wait()
+        stage_sources(coord_tiles(pack_ref, coord_row, leaves // 2), origin, source_ref, place * (leaves // 2))
+        base = place * leaves
+        for leaf in range(leaves):
+            stage_charge(pack_ref[leaf * scen : (leaf + 1) * scen], charge_ref, tail_ref, base + leaf)
     near_pairs(
-        out_ref.shape[0] >= chunk, 0, own_chunks(pairs_ref), out_ref.shape[0], pairs_ref, target_ref, source_ref, charge_ref,
+        leaves >= chunk, 0, chip_chunks(pairs_ref), 0, pairs_ref, target_ref, source_ref, charge_ref,
         tail_ref, out_ref, high_ref, low_ref,
     )
 
@@ -299,7 +317,7 @@
             coef_ref[base + leaf] = pack_ref[coef_place(leaf, scen, rank, panels, coef_row)]
     out_ref[...] = start_ref[...]
     near_pairs(
-        False, own_chunks(pairs_ref), pairs_ref.shape[1] // chunk, 0, pairs_ref, target_ref, source_ref,
+        False, chip_chunks(pairs_ref), pairs_ref.shape[1] // chunk, 0, pairs_ref, target_ref, source_ref,
         charge_ref, tail_ref, out_ref, high_ref, low_ref,
     )
     for copy in copies[3:]:
@@ -357,26 +375,23 @@
     count = near_list.size
     pack_rows = leaves * scen + leaves * lines + leaves * scen * rank // panels
 
-    def stages(places):
-        return (
-            pltpu.VMEM((places * leaves // 2, panels, depth), bf16),
-            pltpu.VMEM((places * leaves, 2 * scen, panels), bf16),
-            pltpu.VMEM((places * leaves, 2 * scen, panels), wide),
-        )
-
+    staged = [
+        pltpu.VMEM((2 * leaves, depth, panels), bf16),
+        pltpu.VMEM((3 * leaves // 2, panels, depth), bf16),
+        pltpu.VMEM((3 * leaves, 2 * scen, panels), bf16),
+        pltpu.VMEM((3 * leaves, 2 * scen, panels), wide),
+    ]
     slots = [pltpu.VMEM((chunk, panels, panels), kind) for kind in (bf16, fine)]
     terms_shape = (branches, clusters, scen // 2, 2 * rank)
-    pack, terms, pairs, target, *own_stages = pl.pallas_call(
+    pack, terms, pairs = pl.pallas_call(
         prep_kernel,
         out_shape=(
             jax.ShapeDtypeStruct((pack_rows, panels), f32),
             jax.ShapeDtypeStruct(terms_shape, f32),
             jax.ShapeDtypeStruct((8, count), jnp.int32),
-            pltpu.VMEM((2 * leaves, depth, panels), bf16),
-            *stages(1),
         ),
         in_specs=[smem] * 2 + [vmem] * 8,
-        out_specs=(vmem,) * 7,
+        out_specs=(vmem,) * 3,
         compiler_params=large,
         name="prep",
     )(
@@ -402,15 +417,21 @@
     stay = functools.partial(pltpu.with_memory_space_constraint, memory_space=pltpu.HBM)
     pairs = stay(pairs)
     near_part = pl.pallas_call(
-        own_kernel,
+        chip_kernel,
         out_shape=kept,
-        in_specs=[smem] + [vmem] * 4,
+        in_specs=[smem] * 2 + [anywhere] * 2,
         out_specs=vmem,
-        scratch_shapes=slots,
+        scratch_shapes=[
+            pltpu.VMEM(pack.shape, f32),
+            pltpu.VMEM(pack.shape, f32),
+            *staged,
+            *slots,
+            pltpu.SemaphoreType.DMA((2,)),
+        ],
         compiler_params=params,
         cost_estimate=cost(10),
-        name="near_own",
-    )(pairs, target, *own_stages)
+        name="near_chip",
+    )(cluster_idx, pairs, stay(pack), chip)
     operands = (
         stay(pack), chip, side, stay(leaf_coupling), terms, stay(up_transfer), stay(down_transfer),
         stay(sibling_coupling), stay(branch_coupling), stay(leaf_down), stay(row_basis),
@@ -422,8 +443,7 @@
         out_specs=vmem,
         scratch_shapes=[
             *(pltpu.VMEM(operand.shape, f32) for operand in operands),
-            pltpu.VMEM((2 * leaves, depth, panels), bf16),
-            *stages(3),
+            *staged,
             pltpu.VMEM((3 * leaves, scen, rank), f32),
             *slots,
             pltpu.SemaphoreType.DMA((len(operands),)),

time: 41.6 us -> 41.6 us (level)
  Pallas kernels: 29.4 us -> 31.3 us
  waiting for transfers between devices: 1.89 us -> 0.01 us
    pallas_call x1, Pallas kernels: 6.33 us -> 11.3 us  [on_device(): pl.pallas_call(chip_kernel, out_shape=kept, in_specs=[smem] * 2 + [anywhe...]
    ppermute x1, starting transfers between devices: 4.37 us -> 0.45 us  [on_device(): chip = lax.ppermute(pack, 'cluster', [(i, i ^ 1) for i in range(clusters)])]
    all_to_all x1, starting transfers between devices: 4.89 us -> 8.7 us  [on_device(): terms = lax.all_to_all(terms, ('branch', 'cluster'), 0, 0, tiled=True)]
    pallas_call x1, Pallas kernels: 19.5 us -> 16.5 us  [on_device(): pl.pallas_call(rest_kernel, out_shape=jax.ShapeDtypeStruct((leaves, scen,...]
    all_to_all x1, waiting for transfers between devices: 1.89 us -> 0.01 us  [on_device(): terms = lax.all_to_all(terms, ('branch', 'cluster'), 0, 0, tiled=True)]
  transfers between devices with their start and end apart: 3 -> 3, of which waited for: 1 -> 0; matrix products, arithmetic and copies ran while one was open for 0% -> 0% of each run, Pallas kernels for 15% -> 27%
where the time goes in v5:
time: 41.6 us; the launch traced here: 41.2 us
  Pallas kernels  31.3 us (75%)
  starting transfers between devices  9.82 us (24%)
    pallas_call x1, Pallas kernels, on_device(): pl.pallas_call(rest_kernel, out_shape=jax.ShapeDtypeStruct((leaves, scen,...  16.5 us
    pallas_call x1, Pallas kernels, on_device(): pl.pallas_call(chip_kernel, out_shape=kept, in_specs=[smem] * 2 + [anywhe...  11.3 us
    all_to_all x1, starting transfers between devices, on_device(): terms = lax.all_to_all(terms, ('branch', 'cluster'), 0, 0, tiled=True)  8.7 us
    pallas_call x1, Pallas kernels, on_device(): pl.pallas_call(prep_kernel, out_shape=(jax.ShapeDtypeStruct((pack_rows, p...  3.57 us
  transfers between devices with their start and end apart: 3, of which 0 were waited for; matrix products, arithmetic and copies ran while one was open for 0% of the time, Pallas kernels for 27%

profile of v5, /device:TPU:0, one launch (start us, length us, event | category | flops | bytes accessed | tf_op | source)
XLA Modules:
  0.0 41.2 jit_solution(18433407948225718800)
XLA Ops:
  0.0 3.6 %prep.1 = (f32[384,256]{1,0:T(8,128)}, f32[2,16,8,128]{3,2,1,0:T(8,128)}, s32[8,256]{1,0:T(8,128)}) custom-call(s32[1]{0:T(128)} %bitcast.cluster_ref, s32[1]{0:T(128)} %bitcast.1.branch_ref.branch_idx_ref, f32[16,16,256]{2,1,0:T(8,128)} %charges_ref.1, f32[3,16,256]{2,1,0:T(8,128)} %bitcast.8, f32[16,256]{1,0:T(8,128)} %areas_ref.1, ...), custom_call_target="tpu_custom_call" | custom-call | tf_op jit(solution)/shard_map/prep/pallas_call | solution.py:386
  3.6 0.5 %collective-permute-start = (f32[384,256]{1,0:T(8,128)}, f32[384,256]{1,0:T(8,128)S(1)}, u32[]{:S(2)}, u32[]{:S(2)}) collective-permute-start(f32[384,256]{1,0:T(8,128)} %get-tuple-element.9.own_any), channel_id=1, source_target_pairs={{0,1},{1,0},{2,3},{3,2},{4,5},{5,4},{6,7},{7,6},{8,9},{9,8},{10,11... | collective-permute-start | bytes 1179656 | tf_op jit(solution)/shard_map/ppermute | solution.py:402
  4.0 0.7 %collective-permute-start.1 = (f32[384,256]{1,0:T(8,128)}, f32[384,256]{1,0:T(8,128)S(1)}, u32[]{:S(2)}, u32[]{:S(2)}) collective-permute-start(f32[384,256]{1,0:T(8,128)} %get-tuple-element.9.own_any), channel_id=1, source_target_pairs={{1,2},{3,4},{5,6},{7,8},{9,10},{11,12},{13,14},{2,1},{4,3},{6,5},{... | collective-permute-start | bytes 1179656 | tf_op jit(solution)/shard_map/ppermute | solution.py:404
  4.7 8.7 %all-to-all-start = ((f32[32,8,128]{2,1,0:T(8,128)}), f32[32,8,128]{2,1,0:T(8,128)S(1)}, u32[]{:S(2)}, u32[]{:S(2)}) async-start(f32[32,8,128]{2,1,0:T(8,128)} %bitcast.7), calls=%async_computation | async-start | bytes 262144 | tf_op jit(solution)/shard_map/all_to_all | solution.py:406
  13.4 0.0 collective-permute-done.chip_any
  13.4 11.3 %near_chip.1.start_ref = f32[16,16,256]{2,1,0:T(8,128)S(1)} custom-call(s32[1]{0:T(128)} %bitcast.cluster_ref, s32[8,256]{1,0:T(8,128)} %get-tuple-element.8.pairs_ref, f32[384,256]{1,0:T(8,128)} %get-tuple-element.9.own_any, f32[384,256]{1,0:T(8,128)S(1)} %collective-permute-done.chip_any), custom_call_target="tpu_custom_call" | custom-call | flops 13421772800 | bytes 1048576 | tf_op jit(solution)/shard_map/near_chip/pallas_call | solution.py:419
  24.8 0.0 all-to-all-done
  24.8 0.0 collective-permute-done.1.side_any
  24.8 16.5 %near_rest.1 = f32[16,16,256]{2,1,0:T(8,128)} custom-call(s32[1]{0:T(128)} %bitcast.cluster_ref, s32[1]{0:T(128)} %bitcast.1.branch_ref.branch_idx_ref, s32[8,256]{1,0:T(8,128)} %get-tuple-element.8.pairs_ref, f32[384,256]{1,0:T(8,128)} %get-tuple-element.9.own_any, f32[384,256]{1,0:T(8,128)S(1)} %collective-permute-done.chip_any, ...), custom_call_target="tpu_custom_call" | custom-call | flops 13421772800 | bytes 1048576 | tf_op jit(solution)/shard_map/near_rest/pallas_call | solution.py:439
Async XLA Ops:
  3.6 9.8 %collective-permute-start = (f32[384,256]{1,0:T(8,128)}, f32[384,256]{1,0:T(8,128)S(1)}, u32[]{:S(2)}, u32[]{:S(2)}) collective-permute-start(f32[384,256]{1,0:T(8,128)} %get-tuple-element.9.own_any), channel_id=1, source_target_pairs={{0,1},{1,0},{2,3},{3,2},{4,5},{5,4},{6,7},{7,6},{8,9},{9,8},{10,11... | collective-permute-start | bytes 1179656 | tf_op jit(solution)/shard_map/ppermute | solution.py:402
  4.0 20.7 %collective-permute-start.1 = (f32[384,256]{1,0:T(8,128)}, f32[384,256]{1,0:T(8,128)S(1)}, u32[]{:S(2)}, u32[]{:S(2)}) collective-permute-start(f32[384,256]{1,0:T(8,128)} %get-tuple-element.9.own_any), channel_id=1, source_target_pairs={{1,2},{3,4},{5,6},{7,8},{9,10},{11,12},{13,14},{2,1},{4,3},{6,5},{... | collective-permute-start | bytes 1179656 | tf_op jit(solution)/shard_map/ppermute | solution.py:404
  4.7 20.0 %all-to-all-start = ((f32[32,8,128]{2,1,0:T(8,128)}), f32[32,8,128]{2,1,0:T(8,128)S(1)}, u32[]{:S(2)}, u32[]{:S(2)}) async-start(f32[32,8,128]{2,1,0:T(8,128)} %bitcast.7), calls=%async_computation | async-start | bytes 262144 | tf_op jit(solution)/shard_map/all_to_all | solution.py:406
